TPU v7x, 32 devices: a whole 2x2x4 slice. The times are simulated.
32 devices in a mesh: groups: 2 (over y), tensor: 4 (over z), dp: 4 (over x, core).
Axes of the slice: x: 2, y: 2, z: 4, core: 2. Of those that a mesh axis runs over, the one named last changes fastest.
Arguments:
- tokens: bfloat16 [1024, 8192], P(('groups', 'dp'), 'tensor'), parts along dimension 0, may hold values from -6 to 6
- in_weight: bfloat16 [8192, 2, 8192], P('dp', None, 'tensor'), may hold values from -0.0625 to 0.0625
- conv_weight: float32 [4, 8192], P(None, 'tensor'), may hold values from -3 to 3
- conv_bias: float32 [8192], P('tensor'), may hold values from -3 to 3
- conv_state: bfloat16 [3, 1024, 8192], P(None, ('groups', 'dp'), 'tensor'), parts along dimension 1, may hold values from -6 to 6
- x_weight: bfloat16 [8192, 544], P('tensor'), may hold values from -0.0625 to 0.0625
- dt_weight: bfloat16 [512, 8192], P(None, 'tensor'), may hold values from -0.25 to 0.25
- dt_bias: float32 [8192], P('tensor'), may hold values from -6.9 to -2.3
- a_log: float32 [16, 8192], P(None, 'tensor'), may hold values from 0 to 2.77
- d_skip: float32 [8192], P('tensor'), may hold values from 0.5 to 1.5
- ssm_state: bfloat16 [1024, 16, 8192], P(('groups', 'dp'), None, 'tensor'), parts along dimension 0, may hold values from -6 to 6
- out_weight: bfloat16 [8192, 8192], P('tensor', 'dp'), may hold values from -0.09375 to 0.09375
- mamba_gain: float32 [8192], replicated, may hold values from 0.5 to 1.5
- moe_gain: float32 [8192], replicated, may hold values from 0.5 to 2
- up_weight: bfloat16 [8192, 24576], P(None, ('tensor', 'dp')), may hold values from -0.0625 to 0.0625
- down_weight: bfloat16 [24576, 8192], P(('tensor', 'dp')), may hold values from -0.078125 to 0.078125
- expert_ids: int32 [1024, 2], P(('groups', 'dp')), parts along dimension 0, may hold values from 0 to 15, as said below
- slot_index: int32 [1024, 2], P(('groups', 'dp')), parts along dimension 0, may hold values from 0 to 64, as said below
- counts: int32 [32], P('groups'), parts along dimension 0, may hold values from 0 to 64, as said below
- route_weight: float32 [1024, 2], P(('groups', 'dp')), parts along dimension 0, may hold values from 0.2 to 1
Outputs:
- mixed: bfloat16 [1024, 8192], P(('groups', 'dp'), 'tensor'), parts along dimension 0
There are 2 independent parts, one for each index of `groups`. A program takes and returns all parts, laid end to end along the dimension named above; an argument that names none is the same for every part. Nothing has to cross between parts.
Inputs may be any that keep to these rules, and one draw needn't show every extreme that they name: `expert_ids`: the two experts of a request differ. Some expert below 2 is named by 64 rows or more. `slot_index`: rows naming one expert are numbered 0, 1, 2 in order of request and then of k; numbers of 64 or more are given as 64. counts[e] is at most the number of rows naming e with slot under 64; for some expert below 2 it is 64.
All inputs are finite; a program needn't handle non-finite values.
Results may differ from a plain program's by a relative error of at most 0.019.
Values may be sent and summed in bfloat16 or wider, within the bound.
A program may use at most 384 MiB of HBM per device.

v0:
```python
import jax
import jax.numpy as jnp
from jax import lax
from jax.sharding import PartitionSpec as P

NSTATE = 16
RANK = 512
EXPERTS = 16
TOP = 2
EXP_WIN = 2


EPS = 1e-05


def shards(
    tokens,
    in_weight,
    conv_weight,
    conv_bias,
    conv_state,
    x_weight,
    dt_weight,
    dt_bias,
    a_log,
    d_skip,
    ssm_state,
    out_weight,
    mamba_gain,
    moe_gain,
    up_weight,
    down_weight,
    expert_ids,
    slot_index,
    counts,
    route_weight,
):
    req_rows = tokens.shape[0]
    whole = lax.all_gather(tokens, "tensor", axis=1, tiled=True)
    whole32 = whole.astype(jnp.float32)
    normed = (
        whole32 * lax.rsqrt(jnp.mean(whole32 * whole32, -1, keepdims=True) + EPS) * mamba_gain
    ).astype(jnp.bfloat16)
    projected = jnp.einsum(
        "bd,dke->bke",
        normed,
        lax.all_gather(in_weight, "dp", axis=0, tiled=True),
        preferred_element_type=jnp.float32,
    )
    inner_part = projected[:, 0]
    gate_part = projected[:, 1]
    history = conv_state.astype(jnp.float32)
    conv_out = (
        conv_bias
        + conv_weight[3] * inner_part
        + conv_weight[0] * history[0]
        + conv_weight[1] * history[1]
        + conv_weight[2] * history[2]
    )
    activated = jax.nn.silu(conv_out)
    local_inputs = jnp.dot(
        activated.astype(jnp.bfloat16), x_weight, preferred_element_type=jnp.float32
    )
    ssm_inputs = lax.psum(local_inputs.astype(jnp.bfloat16), "tensor").astype(jnp.float32)
    step_low = ssm_inputs[:, :RANK].astype(jnp.bfloat16)
    input_map = ssm_inputs[:, RANK : RANK + NSTATE]
    output_map = ssm_inputs[:, RANK + NSTATE :]
    step_size = jax.nn.softplus(
        jnp.dot(step_low, dt_weight, preferred_element_type=jnp.float32) + dt_bias
    )
    rates = -jnp.exp(a_log)
    readout = d_skip * activated
    for index in range(NSTATE):
        state_row = (
            jnp.exp(step_size * rates[index]) * ssm_state[:, index].astype(jnp.float32)
            + step_size * input_map[:, index : index + 1] * activated
        )
        readout = readout + output_map[:, index : index + 1] * state_row
    gated = (readout * jax.nn.silu(gate_part)).astype(jnp.bfloat16)
    out_terms = jnp.dot(
        gated,
        lax.all_gather(out_weight, "dp", axis=1, tiled=True),
        preferred_element_type=jnp.float32,
    )
    mamba_sum = lax.psum_scatter(
        out_terms.astype(jnp.bfloat16), "tensor", scatter_dimension=1, tiled=True
    ).astype(jnp.float32)
    residual = (tokens.astype(jnp.float32) + mamba_sum).astype(jnp.bfloat16)
    carried = residual.astype(jnp.float32)
    feat_cols = carried.shape[1]
    gain_slice = lax.dynamic_slice_in_dim(
        moe_gain, lax.axis_index("tensor") * feat_cols, feat_cols, 0
    )
    moe_rows = (carried * gain_slice).astype(jnp.bfloat16)
    capacity = req_rows * lax.axis_size("dp") * TOP // EXPERTS
    limit = jnp.sum(
        (expert_ids[:, :, None] == jnp.arange(EXPERTS, dtype=jnp.int32)[None, None, :])
        * counts[None, None, :],
        -1,
    )
    valid = (expert_ids < EXP_WIN) & (slot_index < limit)
    target = jnp.where(valid, expert_ids * capacity + slot_index, EXP_WIN * capacity)
    positions = jnp.arange(EXP_WIN * capacity, dtype=jnp.int32)
    slot_match = (positions[:, None] == target[None, :, 0]) | (
        positions[:, None] == target[None, :, 1]
    )
    local_buffer = jnp.dot(
        slot_match.astype(jnp.bfloat16), moe_rows, preferred_element_type=jnp.float32
    ).reshape(EXP_WIN, capacity, feat_cols)
    buffer = lax.psum(local_buffer.astype(jnp.bfloat16), "dp")
    per_expert = lax.axis_size("tensor") // EXP_WIN
    own_expert = lax.axis_index("tensor") // per_expert
    rows = lax.dynamic_index_in_dim(
        lax.all_gather(buffer, "tensor", axis=2, tiled=True), own_expert, 0, keepdims=False
    )
    pre_act = jnp.dot(rows, up_weight, preferred_element_type=jnp.float32)
    hidden = jax.nn.silu(pre_act).astype(jnp.bfloat16)
    partial_out = jnp.dot(hidden, down_weight, preferred_element_type=jnp.float32)
    expert_mask = (jnp.arange(EXP_WIN, dtype=jnp.int32) == own_expert)[:, None, None]
    spread_term = jnp.where(expert_mask, partial_out[None], jnp.float32(0.0))
    feature_sums = lax.psum_scatter(
        spread_term.astype(jnp.bfloat16), "tensor", scatter_dimension=2, tiled=True
    )
    expert_out = lax.psum(feature_sums, "dp").astype(jnp.float32)
    weights = jnp.where(valid, route_weight, jnp.float32(0.0))
    selector = jnp.where(
        positions[None, :] == target[:, 0:1], weights[:, 0:1], jnp.float32(0.0)
    ) + jnp.where(positions[None, :] == target[:, 1:2], weights[:, 1:2], jnp.float32(0.0))
    moe_sum = jnp.dot(
        selector,
        expert_out.reshape(EXP_WIN * capacity, feat_cols),
        precision=lax.Precision.HIGHEST,
        preferred_element_type=jnp.float32,
    )
    return (carried + moe_sum).astype(jnp.bfloat16)


def solution(mesh):
    placed = (
        P(("groups", "dp"), "tensor"),
        P("dp", None, "tensor"),
        P(None, "tensor"),
        P("tensor"),
        P(None, ("groups", "dp"), "tensor"),
        P("tensor", None),
        P(None, "tensor"),
        P("tensor"),
        P(None, "tensor"),
        P("tensor"),
        P(("groups", "dp"), None, "tensor"),
        P("tensor", "dp"),
        P(),
        P(),
        P(None, ("tensor", "dp")),
        P(("tensor", "dp"), None),
        P(("groups", "dp"), None),
        P(("groups", "dp"), None),
        P("groups"),
        P(("groups", "dp"), None),
    )
    return jax.shard_map(
        shards, mesh=mesh, in_specs=placed, out_specs=P(("groups", "dp"), "tensor"), check_vma=False
    )
```

profile of v0, /device:TPU:0, one launch (start us, length us, event | category | flops | bytes accessed | tf_op | source)
XLA Modules:
  0.0 969.8 jit_solution(9600984282354894250)
XLA Ops:
  6.5 0.0 copy-start
  6.5 0.0 all-gather.5.cloned.1.call-start
  6.5 0.7 all-gather.5.cloned.1.call-update
  7.3 0.0 all-gather.7.cloned.1.call-start
  7.3 17.5 %copy.39 = bf16[2048,2,2048]{2,0,1:T(8,128)(2,1)} copy(bf16[2048,2,2048]{2,1,0:T(2,128)(2,1)} %param.21) | data formatting | bytes 33554432 | tf_op args[1]
  24.8 0.0 all-gather.7.cloned.1.call-update
  24.8 0.0 copy-start.9
  24.8 0.0 copy-start.8
  24.9 0.0 all-reduce.4.cloned.1.call-start
  24.9 3.5 convert_element_type.157
  28.4 0.0 copy-done.9
  28.4 29.2 %all-gather.5.cloned.1.call-done = bf16[128,8192]{1,0:T(8,128)(2,1)} async-done(((bf16[128,2048]{1,0:T(8,128)(2,1)}), bf16[128,8192]{1,0:T(8,128)(2,1)}) %all-gather.5.cloned.1.call-update) | async-done | bytes 2097168 | tf_op jit(solution)/shard_map/all_gather | solution.py:39
  57.6 2.1 fusion
  59.7 0.0 copy-start.11
  59.7 390.9 %all-gather.7.cloned.1.call-done = bf16[8192,2,2048]{2,0,1:T(8,128)(2,1)} async-done(((bf16[2048,2,2048]{2,0,1:T(8,128)(2,1)}), bf16[8192,2,2048]{2,0,1:T(8,128)(2,1)}) %all-gather.7.cloned.1.call-update) | async-done | bytes 67108880 | tf_op jit(solution)/shard_map/all_gather | solution.py:47
  450.6 0.0 copy-done.8
  450.6 23.5 %fusion.5 = f32[128,2,2048]{2,0,1:T(8,128)S(1)} fusion(bf16[8192,2,2048]{2,0,1:T(8,128)(2,1)} %all-gather.7.cloned.1.call-done, bf16[128,8192]{1,0:T(8,128)(2,1)} %all-gather.5.cloned.1.call-done, f32[8192]{0:T(1024)S(1)} %copy-done.8, f32[128]{0:T(128)S(1)} %add_rsqrt_fusion), kind=kOutput, calls=%fused_computation.13 | convolution fusion | flops 8594128896 | bytes 71336448 | tf_op jit(solution)/shard_map/bd,dke->bke/dot_general | solution.py:44
  474.2 0.0 copy-start.2
  474.2 1.3 copy-done.2
  475.5 0.0 copy-done.4
  475.5 0.5 divide_multiply_fusion
  476.0 1.4 convolution_convert_fusion.2
  477.4 0.0 all-reduce.4.cloned.1.call-update
  477.4 0.0 copy-start.7
  477.4 0.0 all-gather.9.cloned.1.call-start
  477.5 0.5 all-gather.9.cloned.1.call-update
  478.0 0.2 reduce-scatter.3.cloned.1.call-start
  478.2 0.1 copy-done.7
  478.3 0.1 fusion.154
  478.4 0.0 copy-start.15
  478.5 0.0 copy-start.16
  478.5 31.6 %fusion.153 = (bf16[128,1,2048]{2,1,0:T(2,128)(2,1)}, bf16[128,1,2048]{2,1,0:T(2,128)(2,1)}, bf16[128,1,2048]{2,1,0:T(2,128)(2,1)}, bf16[128,1,2048]{2,1,0:T(2,1...) fusion(bf16[128,16,2048]{2,1,0:T(8,128)(2,1)} %param.30), kind=kLoop, calls=%fused_computation.241 | loop fusion | bytes 16777216 | tf_op jit(solution)/shard_map/slice | solution.py:75
  510.1 1.8 all-reduce.4.cloned.1.call-done
  511.9 0.9 convert_element_type.160
  512.9 15.7 %fusion.172 = bf16[128,2048]{1,0:T(8,128)(2,1)} fusion(f32[128,2,2048]{2,0,1:T(8,128)S(1)} %copy-done.3, f32[128,2048]{1,0:T(8,128)S(1)} %divide_multiply_fusion, bf16[512,2048]{1,0:T(8,128)(2,1)} %param.26, bf16[128,1,2048]{2,1,0:T(2,128)(2,1)} %get-tuple-element.20, bf16[128,1,2048]{2,1,0:T(2,128)(2,1)} %get-tuple-element.6, ...), kind=kOutput, calls=%fused_computation.37.clone.clone.1 | convolution fusion | flops 305659904 | bytes 21790720 | tf_op jit(solution)/shard_map/dot_general | solution.py:69
  528.5 0.0 copy-start.10
  528.5 0.0 copy-start.14
  528.6 0.0 copy-start.12
  528.6 0.0 copy-start.5
  528.6 186.4 %all-gather.9.cloned.1.call-done = bf16[2048,8192]{1,0:T(8,128)(2,1)} async-done(((bf16[2048,2048]{1,0:T(8,128)(2,1)}), bf16[2048,8192]{1,0:T(8,128)(2,1)}) %all-gather.9.cloned.1.call-update) | async-done | bytes 33554448 | tf_op jit(solution)/shard_map/all_gather | solution.py:82
  714.9 16.5 %convolution_convert_fusion = bf16[128,8192]{1,0:T(8,128)(2,1)} fusion(bf16[2048,8192]{1,0:T(8,128)(2,1)} %all-gather.9.cloned.1.call-done, bf16[128,2048]{1,0:T(8,128)(2,1)} %fusion.172), kind=kOutput, calls=%fused_computation | convolution fusion | flops 4296015872 | bytes 36175872 | tf_op jit(solution)/shard_map/dot_general | solution.py:80
  731.5 0.0 reduce-scatter.3.cloned.1.call-update
  731.5 0.0 all-reduce.6.cloned.1.call-start
  731.6 0.7 dynamic_slice.7
  732.3 0.0 copy-done.10
  732.3 0.1 select_reduce_fusion
  732.4 43.2 %reduce-scatter.3.cloned.1.call-done = bf16[128,2048]{1,0:T(8,128)(2,1)} async-done(((bf16[128,8192]{1,0:T(8,128)(2,1)}), bf16[128,2048]{1,0:T(8,128)(2,1)}) %reduce-scatter.3.cloned.1.call-update) | async-done | bytes 524304 | tf_op jit(solution)/shard_map/reduce_scatter | solution.py:85
  775.5 2.2 convolution_convert_fusion.1
  777.7 0.0 all-reduce.6.cloned.1.call-update
  777.7 0.0 all-gather.11.cloned.1.call-start
  777.8 32.6 %all-reduce.6.cloned.1.call-done = bf16[2,64,2048]{2,1,0:T(8,128)(2,1)} async-done(((bf16[2,64,2048]{2,1,0:T(8,128)(2,1)}), bf16[2,64,2048]{2,1,0:T(8,128)(2,1)}) %all-reduce.6.cloned.1.call-update) | async-done | bytes 524304 | tf_op jit(solution)/shard_map/psum | solution.py:110
  810.4 0.0 all-gather.11.cloned.1.call-update
  810.4 0.0 reduce-scatter.5.cloned.1.call-start
  810.5 47.4 %all-gather.11.cloned.1.call-done = bf16[2,64,8192]{2,1,0:T(8,128)(2,1)} async-done(((bf16[2,64,2048]{2,1,0:T(8,128)(2,1)}), bf16[2,64,8192]{2,1,0:T(8,128)(2,1)}) %all-gather.11.cloned.1.call-update) | async-done | bytes 2097168 | tf_op jit(solution)/shard_map/all_gather | solution.py:114
  857.9 21.9 %fusion.130 = bf16[64,8192]{1,0:T(8,128)(2,1)} fusion(bf16[1536,8192]{1,0:T(8,128)(2,1)} %param.35, bf16[8192,1536]{1,0:T(8,128)(2,1)} %param.34, bf16[2,64,8192]{2,1,0:T(8,128)(2,1)} %all-gather.11.cloned.1.call-done, s32[]{:T(128)S(6)} %select_n.42), kind=kOutput, calls=%fused_computation.174 | convolution fusion | flops 3221716992 | bytes 52428804 | tf_op jit(solution)/shard_map/dot_general | solution.py:118
  879.9 3.1 select_convert_fusion
  882.9 0.0 reduce-scatter.5.cloned.1.call-update
  883.0 0.0 all-reduce.8.cloned.1.call-start
  883.0 42.7 %reduce-scatter.5.cloned.1.call-done = bf16[2,64,2048]{2,1,0:T(8,128)(2,1)} async-done(((bf16[2,64,8192]{2,1,0:T(8,128)(2,1)}), bf16[2,64,2048]{2,1,0:T(8,128)(2,1)}) %reduce-scatter.5.cloned.1.call-update) | async-done | bytes 524304 | tf_op jit(solution)/shard_map/reduce_scatter | solution.py:121
  925.7 0.0 all-reduce.8.cloned.1.call-update
  925.8 35.0 %all-reduce.8.cloned.1.call-done = bf16[128,2048]{1,0:T(8,128)(2,1)} async-done(((bf16[128,2048]{1,0:T(8,128)(2,1)}), bf16[128,2048]{1,0:T(8,128)(2,1)}) %all-reduce.8.cloned.1.call-update) | async-done | bytes 524304 | tf_op jit(solution)/shard_map/psum | solution.py:124
  960.7 0.0 copy-done.6
  960.7 2.5 fusion.3
  963.2 0.0 copy-done.1
  (24 shorter events, 0.1 us)
Async XLA Ops:
  6.5 469.4 %copy-start = (bf16[2048,544]{0,1:T(8,128)(2,1)S(1)}, bf16[2048,544]{0,1:T(8,128)(2,1)}, u32[]{:S(2)}) copy-start(bf16[2048,544]{0,1:T(8,128)(2,1)} %param.25) | copy-start | bytes 6684676
  6.5 51.1 %all-gather.5.cloned.1.call-start = ((), (), s32[]{:S(2)}) async-start(), calls=%async_computation.2 | async-start | bytes 2621440 | tf_op jit(solution)/shard_map/all_gather | solution.py:39
  7.3 443.4 %all-gather.7.cloned.1.call-start = ((), (), s32[]{:S(2)}) async-start(), calls=%async_computation.3 | async-start | bytes 83886080 | tf_op jit(solution)/shard_map/all_gather | solution.py:47
  24.8 3.5 copy-start.9
  24.8 425.8 %copy-start.8 = (f32[8192]{0:T(1024)S(1)}, f32[8192]{0:T(1024)}, u32[]{:S(2)}) copy-start(f32[8192]{0:T(1024)} %param.32) | copy-start | bytes 98308
  24.9 487.0 %all-reduce.4.cloned.1.call-start = ((), (), s32[]{:S(2)}) async-start(), calls=%async_computation.4 | async-start | bytes 278528 | tf_op jit(solution)/shard_map/psum | solution.py:64
  59.7 415.8 %copy-start.11 = (f32[2048]{0:T(1024)S(1)}, f32[2048]{0:T(1024)}, u32[]{:S(2)}) copy-start(f32[2048]{0:T(1024)} %param.23) | copy-start | bytes 24580
  450.6 24.8 %copy-start.4 = (f32[3,128,2048]{2,1,0:T(8,128)S(1)}, f32[3,128,2048]{2,1,0:T(8,128)}, u32[]{:S(2)}) copy-start(f32[3,128,2048]{2,1,0:T(8,128)} %convert_element_type.157) | copy-start | bytes 9437188
  474.2 1.3 copy-start.2
  477.4 0.9 copy-start.7
  477.4 237.5 %all-gather.9.cloned.1.call-start = ((), (), s32[]{:S(2)}) async-start(), calls=%async_computation.5 | async-start | bytes 41943040 | tf_op jit(solution)/shard_map/all_gather | solution.py:82
  478.0 297.5 %reduce-scatter.3.cloned.1.call-start = ((), (), s32[]{:S(2)}) async-start(), calls=%async_computation.6 | async-start | bytes 2621440 | tf_op jit(solution)/shard_map/reduce_scatter | solution.py:85
  478.4 34.4 %copy-start.3 = (f32[128,2,2048]{2,0,1:T(8,128)S(1)}, f32[128,2,2048]{2,0,1:T(8,128)}, u32[]{:S(2)}) copy-start(f32[128,2,2048]{2,0,1:T(8,128)} %copy-done.2) | copy-start | bytes 6291460
  478.4 34.4 %copy-start.15 = (f32[2048]{0:T(1024)S(1)}, f32[2048]{0:T(1024)}, u32[]{:S(2)}) copy-start(f32[2048]{0:T(1024)} %param.27) | copy-start | bytes 24580
  478.5 34.4 %copy-start.16 = (f32[2048]{0:T(1024)S(1)}, f32[2048]{0:T(1024)}, u32[]{:S(2)}) copy-start(f32[2048]{0:T(1024)} %param.29) | copy-start | bytes 24580
  528.5 203.7 %copy-start.10 = (s32[128,2]{0,1:T(2,128)S(1)}, s32[128,2]{0,1:T(2,128)}, u32[]{:S(2)}) copy-start(s32[128,2]{0,1:T(2,128)} %param.36) | copy-start | bytes 3076
  528.5 203.7 %copy-start.14 = (s32[16]{0:T(128)S(1)}, s32[16]{0:T(128)}, u32[]{:S(2)}) copy-start(s32[16]{0:T(128)} %param.38) | copy-start | bytes 196
  528.6 203.8 %copy-start.12 = (s32[128,2]{0,1:T(2,128)S(1)}, s32[128,2]{0,1:T(2,128)}, u32[]{:S(2)}) copy-start(s32[128,2]{0,1:T(2,128)} %param.37) | copy-start | bytes 3076
  528.6 247.0 %copy-start.5 = (bf16[128,2048]{1,0:T(8,128)(2,1)S(1)}, bf16[128,2048]{1,0:T(8,128)(2,1)}, u32[]{:S(2)}) copy-start(bf16[128,2048]{1,0:T(8,128)(2,1)} %param.20) | copy-start | bytes 1572868
  731.5 78.9 %all-reduce.6.cloned.1.call-start = ((), (), s32[]{:S(2)}) async-start(), calls=%async_computation.7 | async-start | bytes 1048576 | tf_op jit(solution)/shard_map/psum | solution.py:110
  777.7 80.2 %all-gather.11.cloned.1.call-start = ((), (), s32[]{:S(2)}) async-start(), calls=%async_computation.8 | async-start | bytes 2621440 | tf_op jit(solution)/shard_map/all_gather | solution.py:114
  810.4 115.3 %reduce-scatter.5.cloned.1.call-start = ((), (), s32[]{:S(2)}) async-start(), calls=%async_computation.9 | async-start | bytes 2621440 | tf_op jit(solution)/shard_map/reduce_scatter | solution.py:121
  857.9 105.3 %copy-start.1 = (bf16[2048,544]{0,1:T(8,128)(2,1)S(1)}, bf16[2048,544]{0,1:T(8,128)(2,1)}, u32[]{:S(2)}) copy-start(bf16[2048,544]{0,1:T(8,128)(2,1)} %param.25) | copy-start | bytes 6684676
  879.8 45.9 %copy-start.13 = (f32[128,2]{0,1:T(2,128)S(1)}, f32[128,2]{0,1:T(2,128)}, u32[]{:S(2)}) copy-start(f32[128,2]{0,1:T(2,128)} %param.39) | copy-start | bytes 3076
  879.9 80.9 %copy-start.6 = (bf16[128,2048]{1,0:T(8,128)(2,1)S(1)}, bf16[128,2048]{1,0:T(8,128)(2,1)}, u32[]{:S(2)}) copy-start(bf16[128,2048]{1,0:T(8,128)(2,1)} %reduce-scatter.3.cloned.1.call-done) | copy-start | bytes 1572868
  883.0 77.8 %all-reduce.8.cloned.1.call-start = ((), (), s32[]{:S(2)}) async-start(), calls=%async_computation.10 | async-start | bytes 1048576 | tf_op jit(solution)/shard_map/psum | solution.py:124
Sparse Core Ops, SparseCore 0:
  8.9 48.6 all-gather.4
  59.2 391.4 all-gather.6
  477.5 34.3 all-reduce.3
  513.4 201.5 all-gather.8
  731.6 43.8 reduce-scatter.2
  777.8 32.4 all-reduce.5
  811.9 45.9 all-gather.10
  883.1 42.5 reduce-scatter.4
  928.2 32.4 all-reduce.7
where the time goes:
time: 970 us
  waiting for transfers between devices  810 us (84%)
  matrix products  83.7 us (9%)
  local copies, waits for them, and re-layouts  51.4 us (5%)
  between operations  13.5 us (1%)
  other arithmetic  10.2 us (1%)
    all_gather x1, waiting for transfers between devices, shards(): lax.all_gather(in_weight, 'dp', axis=0, tiled=True)  391 us
    all_gather x1, waiting for transfers between devices, shards(): lax.all_gather(out_weight, 'dp', axis=1, tiled=True)  186 us
    all_gather x1, waiting for transfers between devices, shards(): lax.all_gather(buffer, 'tensor', axis=2, tiled=True)  47.4 us
    reduce_scatter x1, waiting for transfers between devices, shards(): lax.psum_scatter(out_terms.astype(jnp.bfloat16), 'tensor', scatter_dimens...  43.2 us
    reduce_scatter x1, waiting for transfers between devices, shards(): lax.psum_scatter(spread_term.astype(jnp.bfloat16), 'tensor', scatter_dime...  42.7 us
    psum x1, waiting for transfers between devices, shards(): expert_out = lax.psum(feature_sums, 'dp').astype(jnp.float32)  35 us
    psum x1, waiting for transfers between devices, shards(): buffer = lax.psum(local_buffer.astype(jnp.bfloat16), 'dp')  32.6 us
    slice x1, local copies, waits for them, and re-layouts, shards(): ssm_state[:, index].astype(jnp.float32)  31.6 us
  transfers between devices with their start and end apart: 9, of which 9 were waited for; matrix products, arithmetic and copies ran while one was open for 7% of the time, Pallas kernels for 0%

commit v1 on v0

--- a/solution.py
+++ b/solution.py
@@ -36,17 +36,23 @@
     route_weight,
 ):
     req_rows = tokens.shape[0]
-    whole = lax.all_gather(tokens, "tensor", axis=1, tiled=True)
-    whole32 = whole.astype(jnp.float32)
-    normed = (
-        whole32 * lax.rsqrt(jnp.mean(whole32 * whole32, -1, keepdims=True) + EPS) * mamba_gain
-    ).astype(jnp.bfloat16)
-    projected = jnp.einsum(
-        "bd,dke->bke",
-        normed,
-        lax.all_gather(in_weight, "dp", axis=0, tiled=True),
-        preferred_element_type=jnp.float32,
+    chans = in_weight.shape[2]
+    own32 = tokens.astype(jnp.float32)
+    feats = tokens.shape[1]
+    gain_own = lax.dynamic_slice_in_dim(
+        mamba_gain, lax.axis_index("tensor") * feats, feats, 0
     )
+    scaled = (own32 * gain_own).astype(jnp.bfloat16)
+    square_sum = lax.psum(jnp.sum(own32 * own32, -1, keepdims=True), "tensor")
+    inverse = lax.rsqrt(square_sum / mamba_gain.shape[0] + EPS)
+    whole = lax.all_gather(scaled, "tensor", axis=1, tiled=True)
+    part_rows = lax.all_to_all(whole, "dp", split_axis=1, concat_axis=0, tiled=True)
+    weight = in_weight.reshape(in_weight.shape[0], 2 * chans)
+    terms = jnp.dot(part_rows, weight, preferred_element_type=jnp.float32)
+    projected = lax.psum_scatter(
+        terms.astype(jnp.bfloat16), "dp", scatter_dimension=0, tiled=True
+    ).astype(jnp.float32)
+    projected = (projected * inverse).reshape(req_rows, 2, chans)
     inner_part = projected[:, 0]
     gate_part = projected[:, 1]
     history = conv_state.astype(jnp.float32)
@@ -77,13 +83,13 @@
         )
         readout = readout + output_map[:, index : index + 1] * state_row
     gated = (readout * jax.nn.silu(gate_part)).astype(jnp.bfloat16)
-    out_terms = jnp.dot(
-        gated,
-        lax.all_gather(out_weight, "dp", axis=1, tiled=True),
-        preferred_element_type=jnp.float32,
+    gated_all = lax.all_gather(gated, "dp", axis=0, tiled=True)
+    out_cols = jnp.dot(gated_all, out_weight, preferred_element_type=jnp.float32)
+    out_terms = lax.all_to_all(
+        out_cols.astype(jnp.bfloat16), "dp", split_axis=0, concat_axis=1, tiled=True
     )
     mamba_sum = lax.psum_scatter(
-        out_terms.astype(jnp.bfloat16), "tensor", scatter_dimension=1, tiled=True
+        out_terms, "tensor", scatter_dimension=1, tiled=True
     ).astype(jnp.float32)
     residual = (tokens.astype(jnp.float32) + mamba_sum).astype(jnp.bfloat16)
     carried = residual.astype(jnp.float32)

time: 970 us -> 512 us (0.53)
  waiting for transfers between devices: 810 us -> 312 us
  blocking collectives: 0 us -> 37.8 us
  matrix products: 83.7 us -> 66 us
  local copies, waits for them, and re-layouts: 51.4 us -> 64.9 us
    all_gather x3 -> x2, waiting for transfers between devices: 606 us -> 71.5 us  [the longest x1 48.8 us: shards(): whole = lax.all_gather(scaled, 'tensor', axis=1, tiled=True)]
    psum x1, waiting for transfers between devices: 1.78 us -> 31.6 us  [shards(): lax.psum(local_inputs.astype(jnp.bfloat16), 'tensor').astype(jnp.float32)]
    all_to_all x0 -> x1, blocking collectives: none -> 28.2 us  [shards(): lax.all_to_all(out_cols.astype(jnp.bfloat16), 'dp', split_axis=0, concat_...]
    dot_general x2, matrix products: 40.1 us -> 22.9 us  [the longest x1 14.4 us: shards(): terms = jnp.dot(part_rows, weight, preferred_element_type=jnp.float32)]
    reduce_scatter x1 -> x2, waiting for transfers between devices: 43.2 us -> 43.3 us  [the longest x1 43.3 us: shards(): lax.psum_scatter(out_terms, 'tensor', scatter_dimension=1, tiled=True)]
  transfers between devices with their start and end apart: 9 -> 10, of which waited for: 9 -> 9; matrix products, arithmetic and copies ran while one was open for 7% -> 10% of each run, Pallas kernels for 0% -> 0%
where the time goes in v1:
time: 512 us
  waiting for transfers between devices  312 us (61%)
  matrix products  66 us (13%)
  local copies, waits for them, and re-layouts  64.9 us (13%)
  blocking collectives  37.8 us (7%)
  between operations  13.4 us (3%)
  other arithmetic  11.9 us (2%)
  starting transfers between devices  5.27 us (1%)
    all_gather x1, waiting for transfers between devices, shards(): whole = lax.all_gather(scaled, 'tensor', axis=1, tiled=True)  48.8 us
    all_gather x1, waiting for transfers between devices, shards(): lax.all_gather(buffer, 'tensor', axis=2, tiled=True)  47.3 us
    reduce_scatter x1, waiting for transfers between devices, shards(): lax.psum_scatter(out_terms, 'tensor', scatter_dimension=1, tiled=True)  43.3 us
    reduce_scatter x1, waiting for transfers between devices, shards(): lax.psum_scatter(spread_term.astype(jnp.bfloat16), 'tensor', scatter_dime...  42.7 us
    psum x1, waiting for transfers between devices, shards(): expert_out = lax.psum(feature_sums, 'dp').astype(jnp.float32)  34.8 us
    psum x1, waiting for transfers between devices, shards(): buffer = lax.psum(local_buffer.astype(jnp.bfloat16), 'dp')  32.6 us
    slice x1, local copies, waits for them, and re-layouts, shards(): ssm_state[:, index].astype(jnp.float32)  31.8 us
    psum x1, waiting for transfers between devices, shards(): lax.psum(local_inputs.astype(jnp.bfloat16), 'tensor').astype(jnp.float32)  31.6 us
  transfers between devices with their start and end apart: 10, of which 9 were waited for; matrix products, arithmetic and copies ran while one was open for 10% of the time, Pallas kernels for 0%

profile of v1, /device:TPU:0, one launch (start us, length us, event | category | flops | bytes accessed | tf_op | source)
XLA Modules:
  0.0 511.7 jit_solution(6105701551835108949)
XLA Ops:
  6.5 0.0 copy-start
  6.5 0.0 all-gather.4.cloned.1.call-start
  6.5 0.8 dynamic_slice.10
  7.4 2.0 fusion.3
  9.4 0.0 all-gather.4.cloned.1.call-update
  9.4 48.8 %all-gather.4.cloned.1.call-done = bf16[128,8192]{1,0:T(8,128)(2,1)} async-done(((bf16[128,2048]{1,0:T(8,128)(2,1)}), bf16[128,8192]{1,0:T(8,128)(2,1)}) %all-gather.4.cloned.1.call-update) | async-done | bytes 2097168 | tf_op jit(solution)/shard_map/all_gather | solution.py:48
  58.2 3.1 copy.164
  61.3 4.5 all-to-all-start
  65.8 0.0 reduce-scatter.4.cloned.1.call-start
  65.9 17.3 %copy.102 = bf16[256,8,2,2048]{3,1,2,0:T(8,128)(2,1)} copy(bf16[256,8,2,2048]{3,2,1,0:T(2,128)(2,1)} %bitcast.248) | data formatting | bytes 33554432
  83.1 8.4 %all-to-all-done = bf16[128,4,2048]{2,0,1:T(8,128)(2,1)} async-done(((bf16[128,4,2048]{2,0,1:T(8,128)(2,1)}), bf16[128,4,2048]{2,0,1:T(8,128)(2,1)}, u32[]{:S(2)}, u32[]{:S(2)}) %all-to-all-start) | async-done | bytes 2097184 | tf_op jit(solution)/shard_map/all_to_all | solution.py:49
  91.6 14.4 %convolution_convert_fusion = bf16[512,4096]{1,0:T(8,128)(2,1)} fusion(bf16[512,2048]{1,0:T(8,128)(2,1)} %bitcast.2, bf16[2048,4096]{1,0:T(8,128)(2,1)} %bitcast.249), kind=kOutput, calls=%fused_computation | convolution fusion | flops 8592031744 | bytes 23068672 | tf_op jit(solution)/shard_map/dot_general | solution.py:51
  105.9 0.0 reduce-scatter.4.cloned.1.call-update
  106.0 0.0 copy-start.6
  106.0 0.0 copy-start.5
  106.0 0.0 all-reduce.4.cloned.1.call-start
  106.0 3.5 convert_element_type.162
  109.5 9.6 %psum.28 = f32[128,1]{0,1:T(1,128)S(1)} all-reduce(f32[128,1]{0,1:T(1,128)S(1)} %bitcast.277), channel_id=1, replica_groups=mesh['groups'=2,'tensor'=4,'dp'=4] {'tensor'}, use_global_device_ids=true, to_apply=%region_2.0 | all-reduce | flops 128 | bytes 1024 | tf_op jit(solution)/shard_map/psum | solution.py:46
  119.2 0.0 copy-done.5
  119.2 31.8 %fusion.93 = (bf16[128,1,2048]{2,1,0:T(2,128)(2,1)}, bf16[128,1,2048]{2,1,0:T(2,128)(2,1)}, bf16[128,1,2048]{2,1,0:T(2,128)(2,1)}, bf16[128,1,2048]{2,1,0:T(2,12...) fusion(bf16[128,16,2048]{2,1,0:T(8,128)(2,1)} %param.30), kind=kLoop, calls=%fused_computation.186 | loop fusion | bytes 16777216 | tf_op jit(solution)/shard_map/slice | solution.py:81
  151.0 0.0 reduce-scatter.4.cloned.1.call-done
  151.0 2.9 convert_multiply_fusion
  153.9 4.0 reshape.64
  157.8 5.5 %fusion.94 = (f32[128,1,2048]{2,1,0:T(1,128)S(1)}, f32[128,1,2048]{2,1,0:T(1,128)}) fusion(f32[128,2,2048]{2,1,0:T(2,128)} %reshape.64), kind=kLoop, calls=%fused_computation.187 | loop fusion | bytes 4194304 | tf_op jit(solution)/shard_map/slice | solution.py:56
  163.4 0.0 copy-done.2
  163.4 0.7 divide_multiply_fusion
  164.1 0.0 copy-done
  164.1 0.0 copy-start.12
  164.1 0.0 copy-start.13
  164.1 1.4 convolution_convert_fusion.3
  165.5 0.0 all-reduce.4.cloned.1.call-update
  165.6 0.3 all-gather.6.cloned.1.call-start
  165.8 0.1 fusion.95
  165.9 31.6 %all-reduce.4.cloned.1.call-done = bf16[128,544]{0,1:T(8,128)(2,1)} async-done(((bf16[128,544]{0,1:T(8,128)(2,1)}), bf16[128,544]{0,1:T(8,128)(2,1)}) %all-reduce.4.cloned.1.call-update) | async-done | bytes 139280 | tf_op jit(solution)/shard_map/psum | solution.py:70
  197.6 0.9 convert_element_type.165
  198.6 16.2 %fusion.17 = bf16[128,2048]{1,0:T(8,128)(2,1)} fusion(f32[128,1,2048]{2,1,0:T(1,128)} %get-tuple-element.22, f32[128,2048]{1,0:T(8,128)S(1)} %divide_multiply_fusion, bf16[128,1,2048]{2,1,0:T(2,128)(2,1)} %get-tuple-element.20, bf16[128,1,2048]{2,1,0:T(2,128)(2,1)} %get-tuple-element.6, bf16[128,1,2048]{2,1,0:T(2,128)(2,1)} %get-tuple-element.7, ...), kind=kOutput, calls=%fused_computation.37 | convolution fusion | flops 305659904 | bytes 21790720 | tf_op jit(solution)/shard_map/dot_general | solution.py:75
  214.7 0.0 all-gather.6.cloned.1.call-update
  214.8 0.0 reduce-scatter.6.cloned.1.call-start
  214.8 22.7 %all-gather.6.cloned.1.call-done = bf16[512,2048]{1,0:T(8,128)(2,1)} async-done(((bf16[128,2048]{1,0:T(8,128)(2,1)}), bf16[512,2048]{1,0:T(8,128)(2,1)}) %all-gather.6.cloned.1.call-update) | async-done | bytes 2097168 | tf_op jit(solution)/shard_map/all_gather | solution.py:86
  237.5 8.5 %convolution_convert_fusion.1 = bf16[512,2048]{1,0:T(8,128)(2,1)S(1)} fusion(bf16[512,2048]{1,0:T(8,128)(2,1)} %all-gather.6.cloned.1.call-done, bf16[2048,2048]{1,0:T(8,128)(2,1)} %param.31), kind=kOutput, calls=%fused_computation.3 | convolution fusion | flops 4296015872 | bytes 12582912 | tf_op jit(solution)/shard_map/dot_general | solution.py:87
  246.0 28.2 %all_to_all.38 = bf16[4,128,2048]{2,1,0:T(8,128)(2,1)S(1)} all-to-all(bf16[4,128,2048]{2,1,0:T(8,128)(2,1)S(1)} %bitcast.254), channel_id=1, replica_groups=mesh['groups'=2,'tensor'=4,'dp'=4] {'dp'}, dimensions={0} | all-to-all | bytes 4194304 | tf_op jit(solution)/shard_map/all_to_all | solution.py:88
  274.2 1.6 copy.101
  275.8 0.0 dynamic-slice-start
  275.8 0.0 reduce-scatter.6.cloned.1.call-update
  275.9 0.0 all-reduce.6.cloned.1.call-start
  275.9 0.6 copy-done.7
  276.5 0.1 select_reduce_fusion
  276.6 0.0 copy-done.9
  276.6 43.3 %reduce-scatter.6.cloned.1.call-done = bf16[128,2048]{1,0:T(8,128)(2,1)} async-done(((bf16[128,8192]{1,0:T(8,128)(2,1)}), bf16[128,2048]{1,0:T(8,128)(2,1)}) %reduce-scatter.6.cloned.1.call-update) | async-done | bytes 524304 | tf_op jit(solution)/shard_map/reduce_scatter | solution.py:91
  319.9 2.2 convolution_convert_fusion.2
  322.1 0.0 all-reduce.6.cloned.1.call-update
  322.1 0.0 all-gather.8.cloned.1.call-start
  322.1 32.6 %all-reduce.6.cloned.1.call-done = bf16[2,64,2048]{2,1,0:T(8,128)(2,1)} async-done(((bf16[2,64,2048]{2,1,0:T(8,128)(2,1)}), bf16[2,64,2048]{2,1,0:T(8,128)(2,1)}) %all-reduce.6.cloned.1.call-update) | async-done | bytes 524304 | tf_op jit(solution)/shard_map/psum | solution.py:116
  354.7 0.0 all-gather.8.cloned.1.call-update
  354.8 0.3 reduce-scatter.8.cloned.1.call-start
  355.1 47.3 %all-gather.8.cloned.1.call-done = bf16[2,64,8192]{2,1,0:T(8,128)(2,1)} async-done(((bf16[2,64,2048]{2,1,0:T(8,128)(2,1)}), bf16[2,64,8192]{2,1,0:T(8,128)(2,1)}) %all-gather.8.cloned.1.call-update) | async-done | bytes 2097168 | tf_op jit(solution)/shard_map/all_gather | solution.py:120
  402.4 20.8 %fusion.72 = bf16[64,8192]{1,0:T(8,128)(2,1)S(1)} fusion(bf16[1536,8192]{1,0:T(8,128)(2,1)} %param.35, bf16[8192,1536]{1,0:T(8,128)(2,1)} %param.34, bf16[2,64,8192]{2,1,0:T(8,128)(2,1)} %all-gather.8.cloned.1.call-done, s32[]{:T(128)S(6)} %select_n.43), kind=kOutput, calls=%fused_computation.121 | convolution fusion | flops 3221716992 | bytes 52428804 | tf_op jit(solution)/shard_map/dot_general | solution.py:124
  423.2 1.7 select_convert_fusion
  424.9 0.0 reduce-scatter.8.cloned.1.call-update
  425.0 0.0 all-reduce.8.cloned.1.call-start
  425.0 42.7 %reduce-scatter.8.cloned.1.call-done = bf16[2,64,2048]{2,1,0:T(8,128)(2,1)} async-done(((bf16[2,64,8192]{2,1,0:T(8,128)(2,1)}), bf16[2,64,2048]{2,1,0:T(8,128)(2,1)}) %reduce-scatter.8.cloned.1.call-update) | async-done | bytes 524304 | tf_op jit(solution)/shard_map/reduce_scatter | solution.py:127
  467.7 0.0 all-reduce.8.cloned.1.call-update
  467.8 34.8 %all-reduce.8.cloned.1.call-done = bf16[128,2048]{1,0:T(8,128)(2,1)} async-done(((bf16[128,2048]{1,0:T(8,128)(2,1)}), bf16[128,2048]{1,0:T(8,128)(2,1)}) %all-reduce.8.cloned.1.call-update) | async-done | bytes 524304 | tf_op jit(solution)/shard_map/psum | solution.py:130
  502.6 2.5 fusion
  (29 shorter events, 0.1 us)
Async XLA Ops:
  6.5 157.6 %copy-start = (bf16[2048,544]{0,1:T(8,128)(2,1)S(1)}, bf16[2048,544]{0,1:T(8,128)(2,1)}, u32[]{:S(2)}) copy-start(bf16[2048,544]{0,1:T(8,128)(2,1)} %param.25) | copy-start | bytes 6684676
  6.5 51.7 %all-gather.4.cloned.1.call-start = ((), (), s32[]{:S(2)}) async-start(), calls=%async_computation.5 | async-start | bytes 2621440 | tf_op jit(solution)/shard_map/all_gather | solution.py:48
  61.3 30.2 %all-to-all-start = ((bf16[128,4,2048]{2,0,1:T(8,128)(2,1)}), bf16[128,4,2048]{2,0,1:T(8,128)(2,1)}, u32[]{:S(2)}, u32[]{:S(2)}) async-start(bf16[128,4,2048]{2,0,1:T(8,128)(2,1)} %bitcast.251), calls=%async_computation | async-start | bytes 4194304 | tf_op jit(solution)/shard_map/all_to_all | solution.py:49
  65.8 85.2 %reduce-scatter.4.cloned.1.call-start = ((), (), s32[]{:S(2)}) async-start(), calls=%async_computation.6 | async-start | bytes 5242880 | tf_op jit(solution)/shard_map/reduce_scatter | solution.py:52
  106.0 13.2 %copy-start.6 = (f32[4,2048]{1,0:T(4,128)S(1)}, f32[4,2048]{1,0:T(4,128)}, u32[]{:S(2)}) copy-start(f32[4,2048]{1,0:T(4,128)} %param.22) | copy-start | bytes 98308
  106.0 13.2 %copy-start.5 = (f32[16,2048]{1,0:T(8,128)S(1)}, f32[16,2048]{1,0:T(8,128)}, u32[]{:S(2)}) copy-start(f32[16,2048]{1,0:T(8,128)} %param.28) | copy-start | bytes 393220
  106.0 91.6 %all-reduce.4.cloned.1.call-start = ((), (), s32[]{:S(2)}) async-start(), calls=%async_computation.7 | async-start | bytes 278528 | tf_op jit(solution)/shard_map/psum | solution.py:70
  157.8 5.5 %copy-start.2 = (f32[3,128,2048]{2,1,0:T(8,128)S(1)}, f32[3,128,2048]{2,1,0:T(8,128)}, u32[]{:S(2)}) copy-start(f32[3,128,2048]{2,1,0:T(8,128)} %convert_element_type.162) | copy-start | bytes 9437188
  157.8 5.5 %copy-start.8 = (f32[2048]{0:T(1024)S(1)}, f32[2048]{0:T(1024)}, u32[]{:S(2)}) copy-start(f32[2048]{0:T(1024)} %param.23) | copy-start | bytes 24580
  164.1 34.4 %copy-start.12 = (f32[2048]{0:T(1024)S(1)}, f32[2048]{0:T(1024)}, u32[]{:S(2)}) copy-start(f32[2048]{0:T(1024)} %param.29) | copy-start | bytes 24580
  164.1 34.4 %copy-start.13 = (f32[2048]{0:T(1024)S(1)}, f32[2048]{0:T(1024)}, u32[]{:S(2)}) copy-start(f32[2048]{0:T(1024)} %param.27) | copy-start | bytes 24580
  165.6 72.0 %all-gather.6.cloned.1.call-start = ((), (), s32[]{:S(2)}) async-start(), calls=%async_computation.8 | async-start | bytes 2621440 | tf_op jit(solution)/shard_map/all_gather | solution.py:86
  214.8 105.1 %reduce-scatter.6.cloned.1.call-start = ((), (), s32[]{:S(2)}) async-start(), calls=%async_computation.9 | async-start | bytes 2621440 | tf_op jit(solution)/shard_map/reduce_scatter | solution.py:91
  275.8 0.7 copy-start.7
  275.8 0.7 copy-start.11
  275.8 0.8 copy-start.9
  275.8 44.1 %copy-start.3 = (bf16[128,2048]{1,0:T(8,128)(2,1)S(1)}, bf16[128,2048]{1,0:T(8,128)(2,1)}, u32[]{:S(2)}) copy-start(bf16[128,2048]{1,0:T(8,128)(2,1)} %param.20) | copy-start | bytes 1572868
  275.8 44.1 %dynamic-slice-start = ((f32[8192]{0:T(1024)}, s32[]{:T(128)}), f32[2048]{0:T(1024)S(1)}, s32[]{:S(2)}) async-start(f32[8192]{0:T(1024)} %param.33, s32[]{:T(128)} %select_n.36), calls=%async_computation.14 | async-start | bytes 16896 | tf_op jit(solution)/shard_map/dynamic_slice | solution.py:97
  275.9 78.9 %all-reduce.6.cloned.1.call-start = ((), (), s32[]{:S(2)}) async-start(), calls=%async_computation.10 | async-start | bytes 1048576 | tf_op jit(solution)/shard_map/psum | solution.py:116
  322.1 80.3 %all-gather.8.cloned.1.call-start = ((), (), s32[]{:S(2)}) async-start(), calls=%async_computation.11 | async-start | bytes 2621440 | tf_op jit(solution)/shard_map/all_gather | solution.py:120
  354.8 112.9 %reduce-scatter.8.cloned.1.call-start = ((), (), s32[]{:S(2)}) async-start(), calls=%async_computation.12 | async-start | bytes 2621440 | tf_op jit(solution)/shard_map/reduce_scatter | solution.py:127
  424.9 42.8 %copy-start.10 = (f32[128,2]{0,1:T(2,128)S(1)}, f32[128,2]{0,1:T(2,128)}, u32[]{:S(2)}) copy-start(f32[128,2]{0,1:T(2,128)} %param.39) | copy-start | bytes 3076
  424.9 77.7 %copy-start.4 = (bf16[128,2048]{1,0:T(8,128)(2,1)S(1)}, bf16[128,2048]{1,0:T(8,128)(2,1)}, u32[]{:S(2)}) copy-start(bf16[128,2048]{1,0:T(8,128)(2,1)} %reduce-scatter.6.cloned.1.call-done) | copy-start | bytes 1572868
  424.9 80.2 %copy-start.1 = (bf16[2048,544]{0,1:T(8,128)(2,1)S(1)}, bf16[2048,544]{0,1:T(8,128)(2,1)}, u32[]{:S(2)}) copy-start(bf16[2048,544]{0,1:T(8,128)(2,1)} %param.25) | copy-start | bytes 6684676
  425.0 77.6 %all-reduce.8.cloned.1.call-start = ((), (), s32[]{:S(2)}) async-start(), calls=%async_computation.13 | async-start | bytes 1048576 | tf_op jit(solution)/shard_map/psum | solution.py:130
Sparse Core Ops, SparseCore 0:
  9.5 48.6 all-gather.3
  106.1 42.3 reduce-scatter.3
  165.7 31.8 all-reduce.3
  214.9 22.5 all-gather.5
  276.0 43.8 reduce-scatter.5
  322.2 32.4 all-reduce.5
  356.4 45.9 all-gather.7
  425.1 42.5 reduce-scatter.7
  470.1 32.4 all-reduce.7

commit v2 on v1

--- a/solution.py
+++ b/solution.py
@@ -1,6 +1,8 @@
 import jax
 import jax.numpy as jnp
 from jax import lax
+from jax.experimental import pallas as pl
+from jax.experimental.pallas import tpu as pltpu
 from jax.sharding import PartitionSpec as P
 
 NSTATE = 16
@@ -11,6 +13,72 @@
 
 
 EPS = 1e-05
+
+
+def exchange(x, axis, call_id, out_shape, source, place):
+    n = lax.axis_size(axis)
+
+    def kernel(x_ref, out_ref, own_sem, send_sem, recv_sem):
+        me = lax.axis_index(axis)
+        barrier = pltpu.get_barrier_semaphore()
+        for k in range(1, n):
+            pl.semaphore_signal(
+                barrier,
+                inc=1,
+                device_id={axis: lax.rem(me + k, n)},
+                device_id_type=pl.DeviceIdType.MESH,
+            )
+        pl.semaphore_wait(barrier, n - 1)
+        copies = []
+        for k in range(1, n):
+            peer = lax.rem(me + k, n)
+            copies.append(
+                pltpu.make_async_remote_copy(
+                    src_ref=x_ref.at[source(peer)],
+                    dst_ref=out_ref.at[place(me)],
+                    send_sem=send_sem.at[k],
+                    recv_sem=recv_sem.at[k],
+                    device_id={axis: peer},
+                    device_id_type=pl.DeviceIdType.MESH,
+                )
+            )
+        for copy in copies:
+            copy.start()
+        own = pltpu.make_async_copy(x_ref.at[source(me)], out_ref.at[place(me)], own_sem)
+        own.start()
+        own.wait()
+        for copy in copies:
+            copy.wait()
+
+    return pl.pallas_call(
+        kernel,
+        out_shape=jax.ShapeDtypeStruct(out_shape, x.dtype),
+        in_specs=[pl.BlockSpec(memory_space=pl.ANY)],
+        out_specs=pl.BlockSpec(memory_space=pl.ANY),
+        scratch_shapes=[
+            pltpu.SemaphoreType.DMA,
+            pltpu.SemaphoreType.DMA((n,)),
+            pltpu.SemaphoreType.DMA((n,)),
+        ],
+        compiler_params=pltpu.CompilerParams(collective_id=call_id, has_side_effects=True),
+        name="exchange_%d" % call_id,
+    )(x)
+
+
+def rows_at(size):
+    return lambda i: (pl.ds(pl.multiple_of(i * size, size), size), slice(None))
+
+
+def cols_at(size):
+    return lambda i: (slice(None), pl.ds(pl.multiple_of(i * size, size), size))
+
+
+def block_at(i):
+    return (i,)
+
+
+def whole_at(i):
+    return (slice(None),)
 
 
 def shards(
@@ -37,22 +105,23 @@
 ):
     req_rows = tokens.shape[0]
     chans = in_weight.shape[2]
-    own32 = tokens.astype(jnp.float32)
-    feats = tokens.shape[1]
-    gain_own = lax.dynamic_slice_in_dim(
-        mamba_gain, lax.axis_index("tensor") * feats, feats, 0
-    )
-    scaled = (own32 * gain_own).astype(jnp.bfloat16)
-    square_sum = lax.psum(jnp.sum(own32 * own32, -1, keepdims=True), "tensor")
-    inverse = lax.rsqrt(square_sum / mamba_gain.shape[0] + EPS)
-    whole = lax.all_gather(scaled, "tensor", axis=1, tiled=True)
-    part_rows = lax.all_to_all(whole, "dp", split_axis=1, concat_axis=0, tiled=True)
+    dp = lax.axis_size("dp")
+    n_tensor = lax.axis_size("tensor")
+    whole = lax.all_gather(tokens, "tensor", axis=1, tiled=True)
+    whole32 = whole.astype(jnp.float32)
+    normed = (
+        whole32 * lax.rsqrt(jnp.mean(whole32 * whole32, -1, keepdims=True) + EPS) * mamba_gain
+    ).astype(jnp.bfloat16)
+    in_rows = in_weight.shape[0]
+    part_rows = exchange(
+        normed, "dp", 0, (dp * req_rows, in_rows), cols_at(in_rows), rows_at(req_rows)
+    )
     weight = in_weight.reshape(in_weight.shape[0], 2 * chans)
     terms = jnp.dot(part_rows, weight, preferred_element_type=jnp.float32)
     projected = lax.psum_scatter(
         terms.astype(jnp.bfloat16), "dp", scatter_dimension=0, tiled=True
     ).astype(jnp.float32)
-    projected = (projected * inverse).reshape(req_rows, 2, chans)
+    projected = projected.reshape(req_rows, 2, chans)
     inner_part = projected[:, 0]
     gate_part = projected[:, 1]
     history = conv_state.astype(jnp.float32)
@@ -67,7 +136,13 @@
     local_inputs = jnp.dot(
         activated.astype(jnp.bfloat16), x_weight, preferred_element_type=jnp.float32
     )
-    ssm_inputs = lax.psum(local_inputs.astype(jnp.bfloat16), "tensor").astype(jnp.float32)
+    low = local_inputs.astype(jnp.bfloat16)
+    ssm_inputs = jnp.sum(
+        exchange(low, "tensor", 1, (n_tensor,) + low.shape, whole_at, block_at).astype(
+            jnp.float32
+        ),
+        0,
+    )
     step_low = ssm_inputs[:, :RANK].astype(jnp.bfloat16)
     input_map = ssm_inputs[:, RANK : RANK + NSTATE]
     output_map = ssm_inputs[:, RANK + NSTATE :]
@@ -85,8 +160,14 @@
     gated = (readout * jax.nn.silu(gate_part)).astype(jnp.bfloat16)
     gated_all = lax.all_gather(gated, "dp", axis=0, tiled=True)
     out_cols = jnp.dot(gated_all, out_weight, preferred_element_type=jnp.float32)
-    out_terms = lax.all_to_all(
-        out_cols.astype(jnp.bfloat16), "dp", split_axis=0, concat_axis=1, tiled=True
+    out_chunk = out_weight.shape[1]
+    out_terms = exchange(
+        out_cols.astype(jnp.bfloat16),
+        "dp",
+        2,
+        (req_rows, dp * out_chunk),
+        rows_at(req_rows),
+        cols_at(out_chunk),
     )
     mamba_sum = lax.psum_scatter(
         out_terms, "tensor", scatter_dimension=1, tiled=True
@@ -106,28 +187,61 @@
     )
     valid = (expert_ids < EXP_WIN) & (slot_index < limit)
     target = jnp.where(valid, expert_ids * capacity + slot_index, EXP_WIN * capacity)
-    positions = jnp.arange(EXP_WIN * capacity, dtype=jnp.int32)
+    part_slots = capacity // dp
+    positions = (
+        jnp.arange(EXP_WIN * capacity, dtype=jnp.int32)
+        .reshape(EXP_WIN, dp, part_slots)
+        .transpose(1, 0, 2)
+        .reshape(-1)
+    )
     slot_match = (positions[:, None] == target[None, :, 0]) | (
         positions[:, None] == target[None, :, 1]
     )
     local_buffer = jnp.dot(
         slot_match.astype(jnp.bfloat16), moe_rows, preferred_element_type=jnp.float32
-    ).reshape(EXP_WIN, capacity, feat_cols)
-    buffer = lax.psum(local_buffer.astype(jnp.bfloat16), "dp")
-    per_expert = lax.axis_size("tensor") // EXP_WIN
-    own_expert = lax.axis_index("tensor") // per_expert
-    rows = lax.dynamic_index_in_dim(
-        lax.all_gather(buffer, "tensor", axis=2, tiled=True), own_expert, 0, keepdims=False
-    )
+    ).astype(jnp.bfloat16)
+    part_shape = (dp, EXP_WIN * part_slots, feat_cols)
+    filled = exchange(
+        local_buffer, "dp", 3, part_shape, rows_at(EXP_WIN * part_slots), block_at
+    )
+    filled = jnp.sum(filled.astype(jnp.float32), 0).astype(jnp.bfloat16)
+    per_expert = n_tensor // EXP_WIN
+    features = n_tensor * feat_cols
+    own_rows = exchange(
+        filled,
+        "tensor",
+        4,
+        (part_slots, features),
+        lambda i: rows_at(part_slots)(lax.div(i, per_expert)),
+        cols_at(feat_cols),
+    )
+    rows = exchange(own_rows, "dp", 5, (capacity, features), whole_at, rows_at(part_slots))
     pre_act = jnp.dot(rows, up_weight, preferred_element_type=jnp.float32)
     hidden = jax.nn.silu(pre_act).astype(jnp.bfloat16)
     partial_out = jnp.dot(hidden, down_weight, preferred_element_type=jnp.float32)
-    expert_mask = (jnp.arange(EXP_WIN, dtype=jnp.int32) == own_expert)[:, None, None]
-    spread_term = jnp.where(expert_mask, partial_out[None], jnp.float32(0.0))
-    feature_sums = lax.psum_scatter(
-        spread_term.astype(jnp.bfloat16), "tensor", scatter_dimension=2, tiled=True
-    )
-    expert_out = lax.psum(feature_sums, "dp").astype(jnp.float32)
+    shares = exchange(
+        partial_out.astype(jnp.bfloat16),
+        "dp",
+        6,
+        (dp, part_slots, features),
+        rows_at(part_slots),
+        block_at,
+    )
+    shares = jnp.sum(shares.astype(jnp.float32), 0).astype(jnp.bfloat16)
+    shares = exchange(
+        shares, "tensor", 7, (n_tensor, part_slots, feat_cols), cols_at(feat_cols), block_at
+    )
+    shares = jnp.sum(
+        shares.astype(jnp.float32).reshape(EXP_WIN, per_expert, part_slots, feat_cols), 1
+    ).astype(jnp.bfloat16)
+    expert_out = exchange(
+        shares.reshape(EXP_WIN * part_slots, feat_cols),
+        "dp",
+        8,
+        part_shape,
+        whole_at,
+        block_at,
+    ).astype(jnp.float32)
     weights = jnp.where(valid, route_weight, jnp.float32(0.0))
     selector = jnp.where(
         positions[None, :] == target[:, 0:1], weights[:, 0:1], jnp.float32(0.0)

time: 512 us -> 403 us (0.79)
  waiting for transfers between devices: 312 us -> 111 us
  Pallas kernels: 0 us -> 126 us
  blocking collectives: 37.8 us -> 0 us
  matrix products: 66 us -> 71.9 us
    pallas_call x0 -> x9, Pallas kernels: none -> 126 us  [exchange(): pl.pallas_call(kernel, out_shape=jax.ShapeDtypeStruct(out_shape, x.dtype)...]
    psum x3 -> x0, waiting for transfers between devices: 99.1 us -> none  [the longest x1 34.8 us: shards(): expert_out = lax.psum(feature_sums, 'dp').astype(jnp.float32)]
    all_gather x2 -> x1, waiting for transfers between devices: 96.1 us -> 32.8 us  [shards(): whole = lax.all_gather(tokens, 'tensor', axis=1, tiled=True)]
    reduce_scatter x1 -> x0, waiting for transfers between devices: 42.7 us -> none  [shards(): lax.psum_scatter(spread_term.astype(jnp.bfloat16), 'tensor', scatter_dime...]
    all_to_all x1 -> x0, blocking collectives: 28.2 us -> none  [shards(): lax.all_to_all(out_cols.astype(jnp.bfloat16), 'dp', split_axis=0, concat_...]
    psum x1 -> x0, blocking collectives: 9.61 us -> none  [shards(): square_sum = lax.psum(jnp.sum(own32 * own32, -1, keepdims=True), 'tensor')]
    all_to_all x1 -> x0, waiting for transfers between devices: 8.44 us -> none  [shards(): lax.all_to_all(whole, 'dp', split_axis=1, concat_axis=0, tiled=True)]
    reduce_scatter x1, waiting for transfers between devices: 0.02 us -> 7.49 us  [shards(): lax.psum_scatter(terms.astype(jnp.bfloat16), 'dp', scatter_dimension=0, t...]
  transfers between devices with their start and end apart: 10 -> 4, of which waited for: 9 -> 4; matrix products, arithmetic and copies ran while one was open for 10% -> 14% of each run, Pallas kernels for 0% -> 0%
where the time goes in v2:
time: 403 us; the launch traced here: 402 us
  Pallas kernels  126 us (31%)
  waiting for transfers between devices  111 us (28%)
  matrix products  71.9 us (18%)
  local copies, waits for them, and re-layouts  62.7 us (16%)
  other arithmetic  16.7 us (4%)
  between operations  13.4 us (3%)
    pallas_call x9, Pallas kernels, exchange(): pl.pallas_call(kernel, out_shape=jax.ShapeDtypeStruct(out_shape, x.dtype)...  126 us
    reduce_scatter x1, waiting for transfers between devices, shards(): lax.psum_scatter(out_terms, 'tensor', scatter_dimension=1, tiled=True)  44.7 us
    all_gather x1, waiting for transfers between devices, shards(): whole = lax.all_gather(tokens, 'tensor', axis=1, tiled=True)  32.8 us
    slice x1, local copies, waits for them, and re-layouts, shards(): ssm_state[:, index].astype(jnp.float32)  32.5 us
    all_gather x1, waiting for transfers between devices, shards(): gated_all = lax.all_gather(gated, 'dp', axis=0, tiled=True)  25.1 us
    dot_general x1, matrix products, shards(): jnp.dot(hidden, down_weight, preferred_element_type=jnp.float32)  22.2 us
    dot_general x1, matrix products, shards(): jnp.dot(step_low, dt_weight, preferred_element_type=jnp.float32) + dt_bias  20.1 us
    unnamed x33, local copies, waits for them, and re-layouts  17.5 us
  transfers between devices with their start and end apart: 4, of which 4 were waited for; matrix products, arithmetic and copies ran while one was open for 14% of the time, Pallas kernels for 0%

profile of v2, /device:TPU:0, one launch (start us, length us, event | category | flops | bytes accessed | tf_op | source)
XLA Modules:
  0.0 401.7 jit_solution(9286039960687403784)
XLA Ops:
  6.5 0.0 copy-start
  6.5 0.0 all-gather.3.cloned.1.call-start
  6.5 0.7 all-gather.3.cloned.1.call-update
  7.3 0.0 reduce-scatter.3.cloned.1.call-start
  7.3 0.0 copy-start.7
  7.3 17.5 %copy.137 = bf16[256,8,2,2048]{3,1,2,0:T(8,128)(2,1)} copy(bf16[256,8,2,2048]{3,2,1,0:T(2,128)(2,1)} %bitcast.166) | data formatting | bytes 33554432
  24.8 32.8 %all-gather.3.cloned.1.call-done = bf16[128,8192]{1,0:T(8,128)(2,1)} async-done(((bf16[128,2048]{1,0:T(8,128)(2,1)}), bf16[128,8192]{1,0:T(8,128)(2,1)}) %all-gather.3.cloned.1.call-update) | async-done | bytes 2097168 | tf_op jit(solution)/shard_map/all_gather | solution.py:110
  57.6 2.1 fusion
  59.7 0.0 copy-done.7
  59.7 3.5 fusion.2.x_ref
  63.2 24.9 %exchange_0.1 = bf16[512,2048]{1,0:T(8,128)(2,1)} custom-call(bf16[128,8192]{1,0:T(8,128)(2,1)} %fusion.2.x_ref), custom_call_target="tpu_custom_call" | custom-call | tf_op jit(solution)/shard_map/exchange_0/pallas_call | solution.py:53
  88.1 14.3 %convolution_convert_fusion.1 = bf16[512,4096]{1,0:T(8,128)(2,1)} fusion(bf16[512,2048]{1,0:T(8,128)(2,1)} %exchange_0.1, bf16[2048,4096]{1,0:T(8,128)(2,1)} %bitcast.167), kind=kOutput, calls=%fused_computation.1 | convolution fusion | flops 8592031744 | bytes 23068672 | tf_op jit(solution)/shard_map/dot_general | solution.py:120
  102.4 0.0 reduce-scatter.3.cloned.1.call-update
  102.4 0.2 all-gather.5.cloned.1.call-start
  102.6 3.5 convert_element_type.171
  106.1 0.0 copy-done.8
  106.1 0.0 copy-done.6
  106.2 0.1 fusion.88
  106.3 32.5 %fusion.86 = (bf16[128,1,2048]{2,1,0:T(2,128)(2,1)}, bf16[128,1,2048]{2,1,0:T(2,128)(2,1)}, bf16[128,1,2048]{2,1,0:T(2,128)(2,1)}, bf16[128,1,2048]{2,1,0:T(2,12...) fusion(bf16[128,16,2048]{2,1,0:T(8,128)(2,1)} %param.30), kind=kLoop, calls=%fused_computation.183 | loop fusion | bytes 16777216 | tf_op jit(solution)/shard_map/slice | solution.py:156
  138.8 0.0 copy-start.10
  138.8 7.5 %reduce-scatter.3.cloned.1.call-done = bf16[128,4096]{1,0:T(8,128)(2,1)} async-done(((bf16[512,4096]{1,0:T(8,128)(2,1)}), bf16[128,4096]{1,0:T(8,128)(2,1)}) %reduce-scatter.3.cloned.1.call-update) | async-done | bytes 1048592 | tf_op jit(solution)/shard_map/reduce_scatter | solution.py:121
  146.3 4.1 %reshape.179 = f32[128,2,2048]{2,1,0:T(2,128)} reshape(bf16[128,4096]{1,0:T(8,128)(2,1)} %reduce-scatter.3.cloned.1.call-done) | data formatting | bytes 3145728 | tf_op jit(solution)/shard_map/reshape | solution.py:124
  150.4 5.5 %fusion.87 = (f32[128,1,2048]{2,1,0:T(1,128)S(1)}, f32[128,1,2048]{2,1,0:T(1,128)}) fusion(f32[128,2,2048]{2,1,0:T(2,128)} %reshape.179), kind=kLoop, calls=%fused_computation.184 | loop fusion | bytes 4194304 | tf_op jit(solution)/shard_map/slice | solution.py:125
  155.9 0.0 copy-done.10
  155.9 0.0 copy-done.2
  155.9 0.7 divide_multiply_fusion
  156.7 0.0 copy-done
  156.7 0.0 copy-start.14
  156.7 0.7 convolution_convert_fusion.4
  157.4 0.0 copy-start.15
  157.5 0.8 copy.101.x_ref
  158.3 15.3 %exchange_1.1 = bf16[4,128,544]{2,1,0:T(8,128)(2,1)} custom-call(bf16[128,544]{1,0:T(8,128)(2,1)} %copy.101.x_ref), custom_call_target="tpu_custom_call" | custom-call | tf_op jit(solution)/shard_map/exchange_1/pallas_call | solution.py:53
  173.6 1.2 convert_reduce_fusion
  174.8 0.8 slice_reduce_fusion.31
  175.6 0.6 slice_reduce_fusion.30
  176.2 20.1 %fusion.17 = bf16[128,2048]{1,0:T(8,128)(2,1)} fusion(f32[128,1,2048]{2,1,0:T(1,128)} %get-tuple-element.54, f32[128,2048]{1,0:T(8,128)S(1)} %divide_multiply_fusion, bf16[128,1,2048]{2,1,0:T(2,128)(2,1)} %get-tuple-element.52, bf16[128,1,2048]{2,1,0:T(2,128)(2,1)} %get-tuple-element.38, bf16[128,1,2048]{2,1,0:T(2,128)(2,1)} %get-tuple-element.39, ...), kind=kOutput, calls=%fused_computation.35 | convolution fusion | flops 305659904 | bytes 13926400 | tf_op jit(solution)/shard_map/dot_general | solution.py:150
  196.3 0.0 all-gather.5.cloned.1.call-update
  196.4 0.0 reduce-scatter.5.cloned.1.call-start
  196.4 25.1 %all-gather.5.cloned.1.call-done = bf16[512,2048]{1,0:T(8,128)(2,1)} async-done(((bf16[128,2048]{1,0:T(8,128)(2,1)}), bf16[512,2048]{1,0:T(8,128)(2,1)}) %all-gather.5.cloned.1.call-update) | async-done | bytes 2097168 | tf_op jit(solution)/shard_map/all_gather | solution.py:161
  221.5 9.9 %convolution_convert_fusion.2.x_ref = bf16[512,2048]{1,0:T(8,128)(2,1)} fusion(bf16[512,2048]{1,0:T(8,128)(2,1)} %all-gather.5.cloned.1.call-done, bf16[2048,2048]{1,0:T(8,128)(2,1)} %param.31), kind=kOutput, calls=%fused_computation.8 | convolution fusion | flops 4296015872 | bytes 12582912 | tf_op jit(solution)/shard_map/dot_general | solution.py:162
  231.4 0.0 copy-start.3
  231.4 23.8 %exchange_2.1 = bf16[128,8192]{1,0:T(8,128)(2,1)} custom-call(bf16[512,2048]{1,0:T(8,128)(2,1)} %convolution_convert_fusion.2.x_ref), custom_call_target="tpu_custom_call" | custom-call | tf_op jit(solution)/shard_map/exchange_2/pallas_call | solution.py:53
  255.2 0.0 reduce-scatter.5.cloned.1.call-update
  255.3 0.1 reshape.174
  255.4 0.7 dynamic_slice.3
  256.1 0.0 copy-done.13
  256.1 0.1 select_reduce_fusion
  256.2 0.0 copy-done.12
  256.2 44.7 %reduce-scatter.5.cloned.1.call-done = bf16[128,2048]{1,0:T(8,128)(2,1)} async-done(((bf16[128,8192]{1,0:T(8,128)(2,1)}), bf16[128,2048]{1,0:T(8,128)(2,1)}) %reduce-scatter.5.cloned.1.call-update) | async-done | bytes 524304 | tf_op jit(solution)/shard_map/reduce_scatter | solution.py:172
  300.9 0.0 copy-done.3
  300.9 2.2 convolution_convert_fusion.3.x_ref
  303.1 8.0 %exchange_3.1 = bf16[4,32,2048]{2,1,0:T(8,128)(2,1)} custom-call(bf16[128,2048]{1,0:T(8,128)(2,1)} %convolution_convert_fusion.3.x_ref), custom_call_target="tpu_custom_call" | custom-call | tf_op jit(solution)/shard_map/exchange_3/pallas_call | solution.py:53
  311.1 1.8 reduce_sum.63.x_ref
  312.9 9.1 %exchange_4.1.x_ref = bf16[16,8192]{1,0:T(8,128)(2,1)} custom-call(bf16[32,2048]{1,0:T(8,128)(2,1)} %reduce_sum.63.x_ref), custom_call_target="tpu_custom_call" | custom-call | tf_op jit(solution)/shard_map/exchange_4/pallas_call | solution.py:53
  322.0 12.9 %exchange_5.1 = bf16[64,8192]{1,0:T(8,128)(2,1)} custom-call(bf16[16,8192]{1,0:T(8,128)(2,1)} %exchange_4.1.x_ref), custom_call_target="tpu_custom_call" | custom-call | tf_op jit(solution)/shard_map/exchange_5/pallas_call | solution.py:53
  334.9 0.0 copy-start.1
  334.9 22.2 %convolution_convert_fusion.x_ref = bf16[64,8192]{1,0:T(8,128)(2,1)} fusion(bf16[1536,8192]{1,0:T(8,128)(2,1)} %param.35, bf16[64,8192]{1,0:T(8,128)(2,1)} %exchange_5.1, bf16[8192,1536]{1,0:T(8,128)(2,1)} %param.34), kind=kOutput, calls=%fused_computation | convolution fusion | flops 3222241280 | bytes 52428800 | tf_op jit(solution)/shard_map/dot_general | solution.py:221
  357.1 14.1 %exchange_6.1 = bf16[4,16,8192]{2,1,0:T(8,128)(2,1)} custom-call(bf16[64,8192]{1,0:T(8,128)(2,1)} %convolution_convert_fusion.x_ref), custom_call_target="tpu_custom_call" | custom-call | tf_op jit(solution)/shard_map/exchange_6/pallas_call | solution.py:53
  371.2 2.2 reduce_sum.64.x_ref
  373.3 8.9 %exchange_7.1 = bf16[4,16,2048]{2,1,0:T(8,128)(2,1)} custom-call(bf16[16,8192]{1,0:T(8,128)(2,1)} %reduce_sum.64.x_ref), custom_call_target="tpu_custom_call" | custom-call | tf_op jit(solution)/shard_map/exchange_7/pallas_call | solution.py:53
  382.2 1.7 bitcast_reduce_fusion
  383.9 8.7 %exchange_8.1 = bf16[4,32,2048]{2,1,0:T(8,128)(2,1)} custom-call(bf16[32,2048]{1,0:T(8,128)(2,1)} %bitcast.169), custom_call_target="tpu_custom_call" | custom-call | tf_op jit(solution)/shard_map/exchange_8/pallas_call | solution.py:53
  392.6 2.5 fusion.3
  395.1 0.0 copy-done.1
  (23 shorter events, 0.1 us)
Async XLA Ops:
  6.5 150.1 %copy-start = (bf16[2048,544]{0,1:T(8,128)(2,1)S(1)}, bf16[2048,544]{0,1:T(8,128)(2,1)}, u32[]{:S(2)}) copy-start(bf16[2048,544]{0,1:T(8,128)(2,1)} %param.25) | copy-start | bytes 6684676
  6.5 51.1 %all-gather.3.cloned.1.call-start = ((), (), s32[]{:S(2)}) async-start(), calls=%async_computation.2 | async-start | bytes 2621440 | tf_op jit(solution)/shard_map/all_gather | solution.py:110
  7.3 139.0 %reduce-scatter.3.cloned.1.call-start = ((), (), s32[]{:S(2)}) async-start(), calls=%async_computation.3 | async-start | bytes 5242880 | tf_op jit(solution)/shard_map/reduce_scatter | solution.py:121
  7.3 52.4 %copy-start.7 = (f32[8192]{0:T(1024)S(1)}, f32[8192]{0:T(1024)}, u32[]{:S(2)}) copy-start(f32[8192]{0:T(1024)} %param.32) | copy-start | bytes 98308
  102.4 3.7 copy-start.8
  102.4 3.7 copy-start.6
  102.4 119.1 %all-gather.5.cloned.1.call-start = ((), (), s32[]{:S(2)}) async-start(), calls=%async_computation.4 | async-start | bytes 2621440 | tf_op jit(solution)/shard_map/all_gather | solution.py:161
  138.8 17.2 %copy-start.10 = (f32[2048]{0:T(1024)S(1)}, f32[2048]{0:T(1024)}, u32[]{:S(2)}) copy-start(f32[2048]{0:T(1024)} %param.23) | copy-start | bytes 24580
  150.4 5.5 %copy-start.2 = (f32[3,128,2048]{2,1,0:T(8,128)S(1)}, f32[3,128,2048]{2,1,0:T(8,128)}, u32[]{:S(2)}) copy-start(f32[3,128,2048]{2,1,0:T(8,128)} %convert_element_type.171) | copy-start | bytes 9437188
  156.7 19.5 %copy-start.14 = (f32[2048]{0:T(1024)S(1)}, f32[2048]{0:T(1024)}, u32[]{:S(2)}) copy-start(f32[2048]{0:T(1024)} %param.29) | copy-start | bytes 24580
  157.4 18.7 %copy-start.5 = (bf16[128,1,2048]{2,1,0:T(2,128)(2,1)S(1)}, bf16[128,1,2048]{2,1,0:T(2,128)(2,1)}, u32[]{:S(2)}) copy-start(bf16[128,1,2048]{2,1,0:T(2,128)(2,1)} %get-tuple-element.37) | copy-start | bytes 1572868
  157.4 18.7 %copy-start.15 = (f32[2048]{0:T(1024)S(1)}, f32[2048]{0:T(1024)}, u32[]{:S(2)}) copy-start(f32[2048]{0:T(1024)} %param.27) | copy-start | bytes 24580
  196.4 104.5 %reduce-scatter.5.cloned.1.call-start = ((), (), s32[]{:S(2)}) async-start(), calls=%async_computation.5 | async-start | bytes 2621440 | tf_op jit(solution)/shard_map/reduce_scatter | solution.py:172
  231.4 24.7 %copy-start.9 = (s32[128,2]{0,1:T(2,128)S(1)}, s32[128,2]{0,1:T(2,128)}, u32[]{:S(2)}) copy-start(s32[128,2]{0,1:T(2,128)} %param.36) | copy-start | bytes 3076
  231.4 24.7 %copy-start.13 = (s32[16]{0:T(128)S(1)}, s32[16]{0:T(128)}, u32[]{:S(2)}) copy-start(s32[16]{0:T(128)} %param.38) | copy-start | bytes 196
  231.4 24.8 %copy-start.11 = (s32[128,2]{0,1:T(2,128)S(1)}, s32[128,2]{0,1:T(2,128)}, u32[]{:S(2)}) copy-start(s32[128,2]{0,1:T(2,128)} %param.37) | copy-start | bytes 3076
  231.4 24.8 %copy-start.12 = (f32[128,2]{0,1:T(2,128)S(1)}, f32[128,2]{0,1:T(2,128)}, u32[]{:S(2)}) copy-start(f32[128,2]{0,1:T(2,128)} %param.39) | copy-start | bytes 3076
  231.4 69.5 %copy-start.3 = (bf16[128,2048]{1,0:T(8,128)(2,1)S(1)}, bf16[128,2048]{1,0:T(8,128)(2,1)}, u32[]{:S(2)}) copy-start(bf16[128,2048]{1,0:T(8,128)(2,1)} %param.20) | copy-start | bytes 1572868
  334.9 60.2 %copy-start.1 = (bf16[2048,544]{0,1:T(8,128)(2,1)S(1)}, bf16[2048,544]{0,1:T(8,128)(2,1)}, u32[]{:S(2)}) copy-start(bf16[2048,544]{0,1:T(8,128)(2,1)} %param.25) | copy-start | bytes 6684676
  357.1 35.5 %copy-start.4 = (bf16[128,2048]{1,0:T(8,128)(2,1)S(1)}, bf16[128,2048]{1,0:T(8,128)(2,1)}, u32[]{:S(2)}) copy-start(bf16[128,2048]{1,0:T(8,128)(2,1)} %reduce-scatter.5.cloned.1.call-done) | copy-start | bytes 1572868
Sparse Core Ops, SparseCore 0:
  8.9 48.6 all-gather.2
  102.5 43.6 reduce-scatter.2
  196.5 25.0 all-gather.4
  255.4 45.4 reduce-scatter.4

commit v3 on v2

--- a/solution.py
+++ b/solution.py
@@ -79,6 +79,122 @@
 
 def whole_at(i):
     return (slice(None),)
+
+
+def gather_pairs(x, axis, call_id):
+    n = lax.axis_size(axis)
+    rows = x.shape[0]
+    if n != 4:
+        return exchange(x, axis, call_id, (n * rows,) + x.shape[1:], whole_at, rows_at(rows))
+
+    def kernel(x_ref, out_ref, own_sem, send_sem, recv_sem):
+        me = lax.axis_index(axis)
+        far = lax.rem(me + 2, 4)
+        sibling = me + 1 - 2 * lax.rem(me, 2)
+        barrier = pltpu.get_barrier_semaphore()
+        for peer in (far, sibling):
+            pl.semaphore_signal(
+                barrier, inc=1, device_id={axis: peer}, device_id_type=pl.DeviceIdType.MESH
+            )
+        pl.semaphore_wait(barrier, 2)
+        place = rows_at(rows)
+
+        def send(source, owner, peer, k):
+            return pltpu.make_async_remote_copy(
+                src_ref=source,
+                dst_ref=out_ref.at[place(owner)],
+                send_sem=send_sem.at[k],
+                recv_sem=recv_sem.at[k],
+                device_id={axis: peer},
+                device_id_type=pl.DeviceIdType.MESH,
+            )
+
+        across = send(x_ref, me, far, 0)
+        beside = send(x_ref, me, sibling, 1)
+        across.start()
+        beside.start()
+        own = pltpu.make_async_copy(x_ref, out_ref.at[place(me)], own_sem)
+        own.start()
+        own.wait()
+        across.wait_recv()
+        onward = send(out_ref.at[place(far)], far, sibling, 2)
+        onward.start()
+        across.wait_send()
+        beside.wait()
+        onward.wait()
+
+    return pl.pallas_call(
+        kernel,
+        out_shape=jax.ShapeDtypeStruct((n * rows,) + x.shape[1:], x.dtype),
+        in_specs=[pl.BlockSpec(memory_space=pl.ANY)],
+        out_specs=pl.BlockSpec(memory_space=pl.ANY),
+        scratch_shapes=[
+            pltpu.SemaphoreType.DMA,
+            pltpu.SemaphoreType.DMA((3,)),
+            pltpu.SemaphoreType.DMA((3,)),
+        ],
+        compiler_params=pltpu.CompilerParams(collective_id=call_id, has_side_effects=True),
+        name="gather_%d" % call_id,
+    )(x)
+
+
+def scan_kernel(
+    state_ref, step_ref, act_ref, gate_ref, in_ref, out_map_ref, rates_ref, skip_ref, o_ref, acc_ref
+):
+    rows, chans = act_ref.shape
+    width = min(512, chans)
+    for start in range(0, chans, width):
+        cols = slice(start, start + width)
+        rates = rates_ref[:, cols]
+        for r in range(rows):
+            step = step_ref[r : r + 1, cols]
+            driven = step * act_ref[r : r + 1, cols]
+            new = jnp.exp(step * rates) * state_ref[r, :, cols].astype(jnp.float32)
+            new = new + driven * in_ref[r]
+            acc_ref[r : r + 1, cols] = jnp.sum(out_map_ref[r] * new, 0, keepdims=True)
+    gate = gate_ref[...]
+    readout = skip_ref[...] * act_ref[...] + acc_ref[...]
+    o_ref[...] = (readout * (gate / (1.0 + jnp.exp(-gate)))).astype(o_ref.dtype)
+
+
+def scan(state, step_size, activated, gate, input_map, output_map, rates, d_skip):
+    total, chans = activated.shape
+    rows = 16
+    flat = pl.BlockSpec((rows, chans), lambda i: (i, 0))
+    column = pl.BlockSpec((rows, NSTATE, 1), lambda i: (i, 0, 0))
+    return pl.pallas_call(
+        scan_kernel,
+        grid=(total // rows,),
+        out_shape=jax.ShapeDtypeStruct((total, chans), jnp.bfloat16),
+        in_specs=[
+            pl.BlockSpec((rows, NSTATE, chans), lambda i: (i, 0, 0)),
+            flat,
+            flat,
+            flat,
+            column,
+            column,
+            pl.BlockSpec((NSTATE, chans), lambda i: (0, 0)),
+            pl.BlockSpec((1, chans), lambda i: (0, 0)),
+        ],
+        out_specs=flat,
+        scratch_shapes=[pltpu.VMEM((rows, chans), jnp.float32)],
+        compiler_params=pltpu.CompilerParams(vmem_limit_bytes=32 * 2**20),
+        cost_estimate=pl.CostEstimate(
+            flops=8 * total * NSTATE * chans,
+            bytes_accessed=2 * total * NSTATE * chans,
+            transcendentals=total * NSTATE * chans,
+        ),
+        name="scan",
+    )(
+        state,
+        step_size,
+        activated,
+        gate,
+        input_map[:, :, None],
+        output_map[:, :, None],
+        rates,
+        d_skip[None, :],
+    )
 
 
 def shards(
@@ -150,15 +266,10 @@
         jnp.dot(step_low, dt_weight, preferred_element_type=jnp.float32) + dt_bias
     )
     rates = -jnp.exp(a_log)
-    readout = d_skip * activated
-    for index in range(NSTATE):
-        state_row = (
-            jnp.exp(step_size * rates[index]) * ssm_state[:, index].astype(jnp.float32)
-            + step_size * input_map[:, index : index + 1] * activated
-        )
-        readout = readout + output_map[:, index : index + 1] * state_row
-    gated = (readout * jax.nn.silu(gate_part)).astype(jnp.bfloat16)
-    gated_all = lax.all_gather(gated, "dp", axis=0, tiled=True)
+    gated = scan(
+        ssm_state, step_size, activated, gate_part, input_map, output_map, rates, d_skip
+    )
+    gated_all = gather_pairs(gated, "dp", 9)
     out_cols = jnp.dot(gated_all, out_weight, preferred_element_type=jnp.float32)
     out_chunk = out_weight.shape[1]
     out_terms = exchange(
@@ -215,7 +326,7 @@
         lambda i: rows_at(part_slots)(lax.div(i, per_expert)),
         cols_at(feat_cols),
     )
-    rows = exchange(own_rows, "dp", 5, (capacity, features), whole_at, rows_at(part_slots))
+    rows = gather_pairs(own_rows, "dp", 5)
     pre_act = jnp.dot(rows, up_weight, preferred_element_type=jnp.float32)
     hidden = jax.nn.silu(pre_act).astype(jnp.bfloat16)
     partial_out = jnp.dot(hidden, down_weight, preferred_element_type=jnp.float32)
@@ -234,14 +345,9 @@
     shares = jnp.sum(
         shares.astype(jnp.float32).reshape(EXP_WIN, per_expert, part_slots, feat_cols), 1
     ).astype(jnp.bfloat16)
-    expert_out = exchange(
-        shares.reshape(EXP_WIN * part_slots, feat_cols),
-        "dp",
-        8,
-        part_shape,
-        whole_at,
-        block_at,
-    ).astype(jnp.float32)
+    expert_out = gather_pairs(shares.reshape(EXP_WIN * part_slots, feat_cols), "dp", 8).astype(
+        jnp.float32
+    )
     weights = jnp.where(valid, route_weight, jnp.float32(0.0))
     selector = jnp.where(
         positions[None, :] == target[:, 0:1], weights[:, 0:1], jnp.float32(0.0)

time: 403 us -> 392 us (0.973)
  local copies, waits for them, and re-layouts: 62.7 us -> 34.8 us
  Pallas kernels: 126 us -> 151 us
  matrix products: 71.9 us -> 54.5 us
  waiting for transfers between devices: 111 us -> 121 us
    pallas_call x0 -> x4, Pallas kernels: none -> 45.3 us  [the longest x3 37.6 us: gather_pairs(): pl.pallas_call(kernel, out_shape=jax.ShapeDtypeStruct((n * rows,) + x.sha...]
    slice x5 -> x1, local copies, waits for them, and re-layouts: 39.4 us -> 2.69 us  [shards(): gate_part = projected[:, 1]]
    reduce_scatter x1, waiting for transfers between devices: 7.49 us -> 40.1 us  [shards(): lax.psum_scatter(terms.astype(jnp.bfloat16), 'dp', scatter_dimension=0, t...]
    all_gather x1 -> x0, waiting for transfers between devices: 25.1 us -> none  [shards(): gated_all = lax.all_gather(gated, 'dp', axis=0, tiled=True)]
    pallas_call x9 -> x7, Pallas kernels: 126 us -> 106 us  [exchange(): pl.pallas_call(kernel, out_shape=jax.ShapeDtypeStruct(out_shape, x.dtype)...]
    dot_general x1, matrix products: 20.1 us -> 2.64 us  [shards(): jnp.dot(step_low, dt_weight, preferred_element_type=jnp.float32) + dt_bias]
    unnamed x33 -> x41, local copies, waits for them, and re-layouts: 17.5 us -> 26.2 us
  transfers between devices with their start and end apart: 4 -> 3, of which waited for: 4 -> 3; matrix products, arithmetic and copies ran while one was open for 14% -> 6% of each run, Pallas kernels for 0% -> 0%
where the time goes in v3:
time: 392 us
  Pallas kernels  151 us (39%)
  waiting for transfers between devices  121 us (31%)
  matrix products  54.5 us (14%)
  local copies, waits for them, and re-layouts  34.8 us (9%)
  other arithmetic  17.2 us (4%)
  between operations  13.4 us (3%)
    pallas_call x7, Pallas kernels, exchange(): pl.pallas_call(kernel, out_shape=jax.ShapeDtypeStruct(out_shape, x.dtype)...  106 us
    reduce_scatter x1, waiting for transfers between devices, shards(): lax.psum_scatter(out_terms, 'tensor', scatter_dimension=1, tiled=True)  46.9 us
    reduce_scatter x1, waiting for transfers between devices, shards(): lax.psum_scatter(terms.astype(jnp.bfloat16), 'dp', scatter_dimension=0, t...  40.1 us
    pallas_call x3, Pallas kernels, gather_pairs(): pl.pallas_call(kernel, out_shape=jax.ShapeDtypeStruct((n * rows,) + x.sha...  37.6 us
    all_gather x1, waiting for transfers between devices, shards(): whole = lax.all_gather(tokens, 'tensor', axis=1, tiled=True)  32.8 us
    unnamed x41, local copies, waits for them, and re-layouts  26.2 us
    dot_general x1, matrix products, shards(): jnp.dot(hidden, down_weight, preferred_element_type=jnp.float32)  22.2 us
    dot_general x1, matrix products, shards(): terms = jnp.dot(part_rows, weight, preferred_element_type=jnp.float32)  14.4 us
  transfers between devices with their start and end apart: 3, of which 3 were waited for; matrix products, arithmetic and copies ran while one was open for 6% of the time, Pallas kernels for 0%

profile of v3, /device:TPU:0, one launch (start us, length us, event | category | flops | bytes accessed | tf_op | source)
XLA Modules:
  0.0 391.7 jit_solution(9347404280926179260)
XLA Ops:
  6.5 0.0 copy-start
  6.5 0.0 all-gather.2.cloned.1.call-start
  6.5 0.7 all-gather.2.cloned.1.call-update
  7.3 0.0 reduce-scatter.3.cloned.1.call-start
  7.3 17.4 %copy.69 = bf16[256,8,2,2048]{3,1,2,0:T(8,128)(2,1)} copy(bf16[256,8,2,2048]{3,2,1,0:T(2,128)(2,1)} %bitcast.72) | data formatting | bytes 33554432
  24.8 32.8 %all-gather.2.cloned.1.call-done = bf16[128,8192]{1,0:T(8,128)(2,1)} async-done(((bf16[128,2048]{1,0:T(8,128)(2,1)}), bf16[128,8192]{1,0:T(8,128)(2,1)}) %all-gather.2.cloned.1.call-update) | async-done | bytes 2097168 | tf_op jit(solution)/shard_map/all_gather | solution.py:226
  57.6 2.2 fusion
  59.9 1.9 fusion.2.x_ref
  61.8 24.9 %exchange_0.1 = bf16[512,2048]{1,0:T(8,128)(2,1)} custom-call(bf16[128,8192]{1,0:T(8,128)(2,1)} %fusion.2.x_ref), custom_call_target="tpu_custom_call" | custom-call | tf_op jit(solution)/shard_map/exchange_0/pallas_call | solution.py:53
  86.7 14.4 %convolution_convert_fusion.1 = bf16[512,4096]{1,0:T(8,128)(2,1)} fusion(bf16[512,2048]{1,0:T(8,128)(2,1)} %exchange_0.1, bf16[2048,4096]{1,0:T(8,128)(2,1)} %bitcast.73), kind=kOutput, calls=%fused_computation.1 | convolution fusion | flops 8592031744 | bytes 23068672 | tf_op jit(solution)/shard_map/dot_general | solution.py:236
  101.0 0.0 reduce-scatter.3.cloned.1.call-update
  101.0 0.0 copy-start.12
  101.1 0.0 copy-start.10
  101.1 0.2 reduce-scatter.5.cloned.1.call-start
  101.3 3.4 convert_element_type.72
  104.8 0.0 copy-done.10
  104.8 40.1 %reduce-scatter.3.cloned.1.call-done = bf16[128,4096]{1,0:T(8,128)(2,1)} async-done(((bf16[512,4096]{1,0:T(8,128)(2,1)}), bf16[128,4096]{1,0:T(8,128)(2,1)}) %reduce-scatter.3.cloned.1.call-update) | async-done | bytes 1048592 | tf_op jit(solution)/shard_map/reduce_scatter | solution.py:237
  144.9 2.6 copy.55
  147.5 2.7 fusion.35
  150.2 1.3 copy.67
  151.5 2.7 divide_multiply_fusion.act_ref
  154.2 0.0 copy-done
  154.2 0.7 convolution_convert_fusion.4
  154.9 0.8 copy.57.x_ref
  155.7 15.3 %exchange_1.1 = bf16[4,128,544]{2,1,0:T(8,128)(2,1)} custom-call(bf16[128,544]{1,0:T(8,128)(2,1)} %copy.57.x_ref), custom_call_target="tpu_custom_call" | custom-call | tf_op jit(solution)/shard_map/exchange_1/pallas_call | solution.py:53
  171.1 1.2 convert_reduce_fusion
  172.3 0.0 copy-start.9
  172.3 0.1 slice_bitcast_fusion.3
  172.4 0.6 copy-done.9
  173.0 0.8 copy.61.in_ref
  173.9 0.8 copy.62.out_map_ref
  174.7 2.5 copy.68
  177.2 2.6 compare_select_fusion.step_ref
  179.9 0.0 copy-start.2
  179.9 3.4 copy-done.2
  183.3 7.7 %scan.1.x_ref = bf16[128,2048]{1,0:T(8,128)(2,1)S(1)} custom-call(bf16[128,16,2048]{2,1,0:T(8,128)(2,1)S(1)} %copy-done.2, f32[128,2048]{1,0:T(8,128)S(1)} %compare_select_fusion.step_ref, f32[128,2048]{1,0:T(8,128)S(1)} %divide_multiply_fusion.act_ref, f32[128,2048]{1,0:T(8,128)S(1)} %bitcast.70, f32[128,16,1]{2,1,0:T(8,128)S(1)} %copy.61.in_ref, ...), custom_call_target="tpu_custom_call" | custom-call | flops 33554432 | bytes 8388608 | tf_op jit(solution)/shard_map/scan/pallas_call | solution.py:165
  191.0 0.0 copy-start.4
  191.0 0.8 copy-done.4
  191.8 19.5 %gather_9.1 = bf16[512,2048]{1,0:T(8,128)(2,1)} custom-call(bf16[128,2048]{1,0:T(8,128)(2,1)} %copy-done.4), custom_call_target="tpu_custom_call" | custom-call | tf_op jit(solution)/shard_map/gather_9/pallas_call | solution.py:126
  211.3 9.9 %convolution_convert_fusion.2.x_ref = bf16[512,2048]{1,0:T(8,128)(2,1)} fusion(bf16[512,2048]{1,0:T(8,128)(2,1)} %gather_9.1, bf16[2048,2048]{1,0:T(8,128)(2,1)} %param.31), kind=kOutput, calls=%fused_computation.8 | convolution fusion | flops 4296015872 | bytes 12582912 | tf_op jit(solution)/shard_map/dot_general | solution.py:273
  221.1 0.0 copy-start.7
  221.2 24.9 %exchange_2.1 = bf16[128,8192]{1,0:T(8,128)(2,1)} custom-call(bf16[512,2048]{1,0:T(8,128)(2,1)} %convolution_convert_fusion.2.x_ref), custom_call_target="tpu_custom_call" | custom-call | tf_op jit(solution)/shard_map/exchange_2/pallas_call | solution.py:53
  246.1 0.0 reduce-scatter.5.cloned.1.call-update
  246.1 0.1 reshape.138
  246.2 0.7 dynamic_slice.3
  246.9 0.0 copy-done.17
  246.9 0.1 select_reduce_fusion
  247.0 0.0 copy-done.16
  247.1 46.9 %reduce-scatter.5.cloned.1.call-done = bf16[128,2048]{1,0:T(8,128)(2,1)} async-done(((bf16[128,8192]{1,0:T(8,128)(2,1)}), bf16[128,2048]{1,0:T(8,128)(2,1)}) %reduce-scatter.5.cloned.1.call-update) | async-done | bytes 524304 | tf_op jit(solution)/shard_map/reduce_scatter | solution.py:283
  294.0 0.0 copy-done.7
  294.0 2.2 convolution_convert_fusion.3.x_ref
  296.1 8.0 %exchange_3.1 = bf16[4,32,2048]{2,1,0:T(8,128)(2,1)} custom-call(bf16[128,2048]{1,0:T(8,128)(2,1)} %convolution_convert_fusion.3.x_ref), custom_call_target="tpu_custom_call" | custom-call | tf_op jit(solution)/shard_map/exchange_3/pallas_call | solution.py:53
  304.2 1.8 reduce_sum.63.x_ref
  306.0 9.1 %exchange_4.1.x_ref = bf16[16,8192]{1,0:T(8,128)(2,1)} custom-call(bf16[32,2048]{1,0:T(8,128)(2,1)} %reduce_sum.63.x_ref), custom_call_target="tpu_custom_call" | custom-call | tf_op jit(solution)/shard_map/exchange_4/pallas_call | solution.py:53
  315.1 11.3 %gather_5.1 = bf16[64,8192]{1,0:T(8,128)(2,1)} custom-call(bf16[16,8192]{1,0:T(8,128)(2,1)} %exchange_4.1.x_ref), custom_call_target="tpu_custom_call" | custom-call | tf_op jit(solution)/shard_map/gather_5/pallas_call | solution.py:126
  326.4 0.0 copy-start.1
  326.4 22.2 %convolution_convert_fusion.x_ref = bf16[64,8192]{1,0:T(8,128)(2,1)} fusion(bf16[1536,8192]{1,0:T(8,128)(2,1)} %param.35, bf16[64,8192]{1,0:T(8,128)(2,1)} %gather_5.1, bf16[8192,1536]{1,0:T(8,128)(2,1)} %param.34), kind=kOutput, calls=%fused_computation | convolution fusion | flops 3222241280 | bytes 52428800 | tf_op jit(solution)/shard_map/dot_general | solution.py:332
  348.6 13.6 %exchange_6.1 = bf16[4,16,8192]{2,1,0:T(8,128)(2,1)} custom-call(bf16[64,8192]{1,0:T(8,128)(2,1)} %convolution_convert_fusion.x_ref), custom_call_target="tpu_custom_call" | custom-call | tf_op jit(solution)/shard_map/exchange_6/pallas_call | solution.py:53
  362.2 2.2 reduce_sum.64.x_ref
  364.3 9.7 %exchange_7.1 = bf16[4,16,2048]{2,1,0:T(8,128)(2,1)} custom-call(bf16[16,8192]{1,0:T(8,128)(2,1)} %reduce_sum.64.x_ref), custom_call_target="tpu_custom_call" | custom-call | tf_op jit(solution)/shard_map/exchange_7/pallas_call | solution.py:53
  374.0 1.7 bitcast_reduce_fusion
  375.7 6.9 %gather_8.1 = bf16[128,2048]{1,0:T(8,128)(2,1)} custom-call(bf16[32,2048]{1,0:T(8,128)(2,1)} %bitcast.75), custom_call_target="tpu_custom_call" | custom-call | tf_op jit(solution)/shard_map/gather_8/pallas_call | solution.py:126
  382.6 2.5 fusion.3
  385.1 0.0 copy-done.1
  (29 shorter events, 0.1 us)
Async XLA Ops:
  6.5 147.6 %copy-start = (bf16[2048,544]{0,1:T(8,128)(2,1)S(1)}, bf16[2048,544]{0,1:T(8,128)(2,1)}, u32[]{:S(2)}) copy-start(bf16[2048,544]{0,1:T(8,128)(2,1)} %param.25) | copy-start | bytes 6684676
  6.5 51.1 %all-gather.2.cloned.1.call-start = ((), (), s32[]{:S(2)}) async-start(), calls=%async_computation.2 | async-start | bytes 2621440 | tf_op jit(solution)/shard_map/all_gather | solution.py:226
  7.3 137.6 %reduce-scatter.3.cloned.1.call-start = ((), (), s32[]{:S(2)}) async-start(), calls=%async_computation.3 | async-start | bytes 5242880 | tf_op jit(solution)/shard_map/reduce_scatter | solution.py:237
  7.3 52.5 %copy-start.11 = (f32[8192]{0:T(1024)S(1)}, f32[8192]{0:T(1024)}, u32[]{:S(2)}) copy-start(f32[8192]{0:T(1024)} %param.32) | copy-start | bytes 98308
  57.6 2.3 copy-start.6
  101.0 3.7 copy-start.12
  101.1 3.7 copy-start.10
  101.1 192.9 %reduce-scatter.5.cloned.1.call-start = ((), (), s32[]{:S(2)}) async-start(), calls=%async_computation.4 | async-start | bytes 2621440 | tf_op jit(solution)/shard_map/reduce_scatter | solution.py:283
  147.5 4.0 %copy-start.14 = (f32[2048]{0:T(1024)S(1)}, f32[2048]{0:T(1024)}, u32[]{:S(2)}) copy-start(f32[2048]{0:T(1024)} %param.23) | copy-start | bytes 24580
  155.7 21.5 %copy-start.18 = (f32[2048]{0:T(1024)S(1)}, f32[2048]{0:T(1024)}, u32[]{:S(2)}) copy-start(f32[2048]{0:T(1024)} %param.27) | copy-start | bytes 24580
  172.3 0.7 copy-start.9
  174.7 5.2 %copy-start.5 = (f32[2048]{0:T(1024)S(1)}, f32[2048]{0:T(1024)}, u32[]{:S(2)}) copy-start(f32[2048]{0:T(1024)} %param.29) | copy-start | bytes 24580
  177.2 2.7 copy-start.3
  179.9 3.4 copy-start.2
  191.0 0.8 copy-start.4
  221.1 25.8 %copy-start.13 = (s32[128,2]{0,1:T(2,128)S(1)}, s32[128,2]{0,1:T(2,128)}, u32[]{:S(2)}) copy-start(s32[128,2]{0,1:T(2,128)} %param.36) | copy-start | bytes 3076
  221.1 25.8 %copy-start.17 = (s32[16]{0:T(128)S(1)}, s32[16]{0:T(128)}, u32[]{:S(2)}) copy-start(s32[16]{0:T(128)} %param.38) | copy-start | bytes 196
  221.1 25.9 %copy-start.15 = (s32[128,2]{0,1:T(2,128)S(1)}, s32[128,2]{0,1:T(2,128)}, u32[]{:S(2)}) copy-start(s32[128,2]{0,1:T(2,128)} %param.37) | copy-start | bytes 3076
  221.1 25.9 %copy-start.16 = (f32[128,2]{0,1:T(2,128)S(1)}, f32[128,2]{0,1:T(2,128)}, u32[]{:S(2)}) copy-start(f32[128,2]{0,1:T(2,128)} %param.39) | copy-start | bytes 3076
  221.1 72.8 %copy-start.7 = (bf16[128,2048]{1,0:T(8,128)(2,1)S(1)}, bf16[128,2048]{1,0:T(8,128)(2,1)}, u32[]{:S(2)}) copy-start(bf16[128,2048]{1,0:T(8,128)(2,1)} %param.20) | copy-start | bytes 1572868
  326.4 58.8 %copy-start.1 = (bf16[2048,544]{0,1:T(8,128)(2,1)S(1)}, bf16[2048,544]{0,1:T(8,128)(2,1)}, u32[]{:S(2)}) copy-start(bf16[2048,544]{0,1:T(8,128)(2,1)} %param.25) | copy-start | bytes 6684676
  348.6 34.0 %copy-start.8 = (bf16[128,2048]{1,0:T(8,128)(2,1)S(1)}, bf16[128,2048]{1,0:T(8,128)(2,1)}, u32[]{:S(2)}) copy-start(bf16[128,2048]{1,0:T(8,128)(2,1)} %reduce-scatter.5.cloned.1.call-done) | copy-start | bytes 1572868
Sparse Core Ops, SparseCore 0:
  8.9 48.6 all-gather.1
  101.2 43.6 reduce-scatter.2
  246.2 47.6 reduce-scatter.4
